TPU v7x, 32 devices: a whole 2x2x4 slice. The times are simulated.
32 devices in a mesh: dp: 4 (over y, x), pipe: 2 (over core), seq: 4 (over z).
Axes of the slice: x: 2, y: 2, z: 4, core: 2. Of those that a mesh axis runs over, the one named last changes fastest.
Arguments:
- query_first: bfloat16 [4, 2, 256, 4096], P('dp', 'pipe', 'seq'), may hold values from -5 to 5
- key_first: bfloat16 [4, 2, 256, 512], P('dp', 'pipe', 'seq'), may hold values from -5 to 5
- value_first: bfloat16 [4, 2, 256, 512], P('dp', 'pipe', 'seq'), may hold values from -36 to 36
- query_second: bfloat16 [4, 2, 256, 4096], P('dp', 'pipe', 'seq'), may hold values from -5 to 5
- key_second: bfloat16 [4, 2, 256, 512], P('dp', 'pipe', 'seq'), may hold values from -5 to 5
- value_second: bfloat16 [4, 2, 256, 512], P('dp', 'pipe', 'seq'), may hold values from -36 to 36
- grad_output: bfloat16 [4, 2, 256, 4096], P('dp', 'pipe', 'seq'), may hold values from -6 to 6
- gain: bfloat16 [2, 4096], P('pipe'), may hold values from 0.5 to 1.5
Outputs:
- next_input: bfloat16 [4, 2, 256, 4096], P('dp', 'pipe', 'seq')
- grad_query: bfloat16 [4, 2, 256, 4096], P('dp', 'pipe', 'seq')
- grad_key: bfloat16 [4, 2, 256, 512], P('dp', 'pipe', 'seq')
- grad_value: bfloat16 [4, 2, 256, 512], P('dp', 'pipe', 'seq')
- grad_gain: float32 [2, 4096], P('pipe', 'seq')
All inputs are finite; a program needn't handle non-finite values.
Results may differ from a plain program's by a relative error of at most 0.012.
The roundings to bfloat16 on the way count: a program that leaves them out, or rounds other values in their place, can miss the bound.
Values may be sent and summed in bfloat16 or wider, within the bound.
A program may use at most 64 MiB of HBM per device.

v0:
```python
import math

import jax
import jax.numpy as jnp
from jax import lax
from jax.sharding import PartitionSpec as P

QH = 32
KVH = 4
HD = 128


epsilon = 1e-05


def from_behind(value, axis, steps):
    count = lax.axis_size(axis)
    pairs = [(source, (source + steps) % count) for source in range(count)]
    return lax.ppermute(value, axis, pairs)


def local(
    query_first, key_first, value_first, query_second, key_second, value_second, grad_output, gain
):
    seq_count = lax.axis_size("seq")
    seq_index = lax.axis_index("seq")
    local_heads = QH // seq_count
    kv_share = seq_count // KVH
    kv_index = seq_index // kv_share
    head_width = local_heads * HD
    scaling = 1.0 / math.sqrt(HD)
    gain_row = gain[0].astype(jnp.float32)

    def heads_layout(query, keys, values):
        query_local = lax.all_to_all(query, "seq", split_axis=1, concat_axis=0, tiled=True)
        keys_all, values_all = (
            lax.all_gather(keys, "seq", axis=0, tiled=True),
            lax.all_gather(values, "seq", axis=0, tiled=True),
        )
        keys_local = lax.dynamic_slice_in_dim(keys_all, kv_index * HD, HD, 1)
        values_local = lax.dynamic_slice_in_dim(values_all, kv_index * HD, HD, 1)
        return (query_local, keys_local, values_local)

    def probabilities(query_block, keys, offset):
        block_rows = query_block.shape[0]
        scores = (
            jnp.einsum("ihd,jd->hij", query_block, keys, preferred_element_type=jnp.float32)
            * scaling
        )
        row_ids = offset + lax.iota(jnp.int32, block_rows)
        column_ids = lax.iota(jnp.int32, keys.shape[0])
        allowed = column_ids[None, :] <= row_ids[:, None]
        scores = jnp.where(allowed[None], scores, -jnp.inf)
        highest = jnp.max(scores, axis=-1, keepdims=True)
        exponent = jnp.exp(scores - highest)
        return exponent / jnp.sum(exponent, axis=-1, keepdims=True)

    def causal_forward(query_local, keys_local, values_local):
        length = query_local.shape[0]
        block_rows = min(512, length)
        outputs = []
        for offset in range(0, length, block_rows):
            finish = offset + block_rows
            query_block = query_local[offset:finish].reshape(block_rows, local_heads, HD)
            weights = probabilities(query_block, keys_local[:finish], offset).astype(jnp.bfloat16)
            result = jnp.einsum(
                "hij,jd->ihd", weights, values_local[:finish], preferred_element_type=jnp.float32
            )
            outputs.append(result.reshape(block_rows, head_width).astype(jnp.bfloat16))
        return jnp.concatenate(outputs, axis=0)

    first_query, first_keys, first_values = heads_layout(
        query_first[0, 0], key_first[0, 0], value_first[0, 0]
    )
    first_out = causal_forward(first_query, first_keys, first_values)
    first_tokens = lax.all_to_all(first_out, "seq", split_axis=0, concat_axis=1, tiled=True).astype(
        jnp.float32
    )
    first_inverse = lax.rsqrt(
        jnp.mean(first_tokens * first_tokens, axis=-1, keepdims=True) + epsilon
    )
    sending = (gain_row * first_tokens * first_inverse).astype(jnp.bfloat16)
    next_input = from_behind(sending, "pipe", 1)
    upstream = from_behind(grad_output[0, 0], "pipe", -1)
    second_query, second_keys, second_values = heads_layout(
        query_second[0, 0], key_second[0, 0], value_second[0, 0]
    )
    second_out = causal_forward(second_query, second_keys, second_values)
    activity = lax.all_to_all(second_out, "seq", split_axis=0, concat_axis=1, tiled=True).astype(
        jnp.float32
    )
    inverse = lax.rsqrt(jnp.mean(activity * activity, axis=-1, keepdims=True) + epsilon)
    upstream_float = upstream.astype(jnp.float32)
    gained = gain_row * upstream_float
    cross_mean = jnp.mean(gained * activity, axis=-1, keepdims=True)
    grad_tokens = (gained * inverse - activity * inverse**3 * cross_mean).astype(jnp.bfloat16)
    partial_gain = jnp.sum(upstream_float * activity * inverse, axis=0)
    gain_share = lax.psum_scatter(partial_gain, "seq", scatter_dimension=0, tiled=True)
    grad_gain = lax.psum(gain_share, "dp")
    grad_local = lax.all_to_all(grad_tokens, "seq", split_axis=1, concat_axis=0, tiled=True)
    length = second_query.shape[0]
    block_rows = min(512, length)
    grad_keys = jnp.zeros((length, HD), jnp.float32)
    grad_values = jnp.zeros((length, HD), jnp.float32)
    pieces = []
    for offset in range(0, length, block_rows):
        finish = offset + block_rows
        query_block = second_query[offset:finish].reshape(block_rows, local_heads, HD)
        grad_block = grad_local[offset:finish].reshape(block_rows, local_heads, HD)
        output_block = second_out[offset:finish].reshape(block_rows, local_heads, HD)
        probability = probabilities(query_block, second_keys[:finish], offset)
        weights = probability.astype(jnp.bfloat16)
        grad_values = grad_values.at[:finish].add(
            jnp.einsum("hij,ihd->jd", weights, grad_block, preferred_element_type=jnp.float32)
        )
        grad_weights = jnp.einsum(
            "ihd,jd->hij", grad_block, second_values[:finish], preferred_element_type=jnp.float32
        )
        row_dots = jnp.sum(
            grad_block.astype(jnp.float32) * output_block.astype(jnp.float32), axis=-1
        )
        grad_scores = (probability * (grad_weights - row_dots.T[:, :, None]) * scaling).astype(
            jnp.bfloat16
        )
        query_part = jnp.einsum(
            "hij,jd->ihd", grad_scores, second_keys[:finish], preferred_element_type=jnp.float32
        )
        pieces.append(query_part.reshape(block_rows, head_width).astype(jnp.bfloat16))
        grad_keys = grad_keys.at[:finish].add(
            jnp.einsum("hij,ihd->jd", grad_scores, query_block, preferred_element_type=jnp.float32)
        )
    query_grads_local, grad_keys, grad_values = (
        jnp.concatenate(pieces, axis=0),
        grad_keys,
        grad_values,
    )
    grad_query = lax.all_to_all(query_grads_local, "seq", split_axis=0, concat_axis=1, tiled=True)
    key_back, value_back = (
        lax.all_to_all(grad_keys, "seq", split_axis=0, concat_axis=1, tiled=True),
        lax.all_to_all(grad_values, "seq", split_axis=0, concat_axis=1, tiled=True),
    )
    row_count = key_back.shape[0]
    grad_key = (
        key_back.reshape(row_count, KVH, kv_share, HD)
        .sum(axis=2)
        .reshape(row_count, KVH * HD)
        .astype(jnp.bfloat16)
    )
    grad_value = (
        value_back.reshape(row_count, KVH, kv_share, HD)
        .sum(axis=2)
        .reshape(row_count, KVH * HD)
        .astype(jnp.bfloat16)
    )
    return (
        next_input[None, None],
        grad_query[None, None],
        grad_key[None, None],
        grad_value[None, None],
        grad_gain[None],
    )


def solution(mesh):
    return jax.shard_map(
        local,
        mesh=mesh,
        in_specs=(
            P("dp", "pipe", "seq", None),
            P("dp", "pipe", "seq", None),
            P("dp", "pipe", "seq", None),
            P("dp", "pipe", "seq", None),
            P("dp", "pipe", "seq", None),
            P("dp", "pipe", "seq", None),
            P("dp", "pipe", "seq", None),
            P("pipe", None),
        ),
        out_specs=(
            P("dp", "pipe", "seq", None),
            P("dp", "pipe", "seq", None),
            P("dp", "pipe", "seq", None),
            P("dp", "pipe", "seq", None),
            P("pipe", "seq"),
        ),
        check_vma=False,
    )
```

profile of v0, /device:TPU:0, one launch (start us, length us, event | category | flops | bytes accessed | tf_op | source)
XLA Modules:
  0.0 216.6 jit_solution(6753918034212595349)
XLA Ops:
  0.6 1.5 all_to_all.38
  2.1 1.0 copy.76
  3.1 6.4 %all-to-all-start = ((bf16[64,4,1024]{2,0,1:T(8,128)(2,1)}), bf16[64,4,1024]{2,0,1:T(8,128)(2,1)S(1)}, u32[]{:S(2)}, u32[]{:S(2)}) async-start(bf16[64,4,1024]{2,0,1:T(8,128)(2,1)} %copy.76), calls=%async_computation | async-start | bytes 1048576 | tf_op jit(solution)/shard_map/all_to_all | solution.py:35
  9.6 0.4 all_to_all.82
  9.9 1.0 copy.81
  10.9 13.1 %all-to-all-done = bf16[64,4,1024]{2,0,1:T(8,128)(2,1)S(1)} async-done(((bf16[64,4,1024]{2,0,1:T(8,128)(2,1)}), bf16[64,4,1024]{2,0,1:T(8,128)(2,1)S(1)}, u32[]{:S(2)}, u32[]{:S(2)}) %all-to-all-start) | async-done | bytes 524320 | tf_op jit(solution)/shard_map/all_to_all | solution.py:35
  24.0 3.5 %all-to-all-start.2 = ((bf16[64,4,1024]{2,0,1:T(8,128)(2,1)}), bf16[64,4,1024]{2,0,1:T(8,128)(2,1)S(1)}, u32[]{:S(2)}, u32[]{:S(2)}) async-start(bf16[64,4,1024]{2,0,1:T(8,128)(2,1)} %copy.81), calls=%async_computation.2 | async-start | bytes 1048576 | tf_op jit(solution)/shard_map/all_to_all | solution.py:35
  27.5 21.5 %all-gather.2 = bf16[1,1,256,512]{3,2,1,0:T(8,128)(2,1)S(1)} all-gather(bf16[1,1,64,512]{3,2,1,0:T(8,128)(2,1)S(1)} %copy-done.8), channel_id=4, replica_groups=mesh['dp'=4,'pipe'=2,'seq'=4] {'seq'}, dimensions={2}, use_global_device_ids=true | all-gather | bytes 327680 | tf_op jit(solution)/shard_map/all_gather | solution.py:37
  49.1 15.0 %all-gather.3 = bf16[1,1,256,512]{3,2,1,0:T(8,128)(2,1)} all-gather(bf16[1,1,64,512]{3,2,1,0:T(8,128)(2,1)S(1)} %copy-done.9), channel_id=5, replica_groups=mesh['dp'=4,'pipe'=2,'seq'=4] {'seq'}, dimensions={2}, use_global_device_ids=true | all-gather | bytes 327680 | tf_op jit(solution)/shard_map/all_gather | solution.py:38
  64.0 13.9 %all-gather.1 = bf16[1,1,256,512]{3,2,1,0:T(8,128)(2,1)S(1)} all-gather(bf16[1,1,64,512]{3,2,1,0:T(8,128)(2,1)S(1)} %copy-done.10), channel_id=3, replica_groups=mesh['dp'=4,'pipe'=2,'seq'=4] {'seq'}, dimensions={2}, use_global_device_ids=true | all-gather | bytes 327680 | tf_op jit(solution)/shard_map/all_gather | solution.py:37
  78.0 13.9 %all-gather = bf16[1,1,256,512]{3,2,1,0:T(8,128)(2,1)S(1)} all-gather(bf16[1,1,64,512]{3,2,1,0:T(8,128)(2,1)S(1)} %copy-done.11), channel_id=2, replica_groups=mesh['dp'=4,'pipe'=2,'seq'=4] {'seq'}, dimensions={2}, use_global_device_ids=true | all-gather | bytes 327680 | tf_op jit(solution)/shard_map/all_gather | solution.py:38
  91.9 0.1 copy.115
  92.0 0.1 copy.116
  92.1 2.1 fusion.80
  94.3 1.9 fusion.15
  96.2 0.3 copy.79
  96.5 1.0 convert_element_type.127
  97.5 4.4 %all-to-all-start.1 = ((bf16[4,64,1024]{2,1,0:T(8,128)(2,1)}), bf16[4,64,1024]{2,1,0:T(8,128)(2,1)S(1)}, u32[]{:S(2)}, u32[]{:S(2)}) async-start(bf16[4,64,1024]{2,1,0:T(8,128)(2,1)} %convert_element_type.127), calls=%async_computation.1 | async-start | bytes 1048576 | tf_op jit(solution)/shard_map/all_to_all | solution.py:76
  101.9 0.5 fusion.9
  102.3 0.4 fusion.12
  102.8 1.6 fusion.16
  104.4 1.1 copy.85
  105.5 2.1 convert_element_type.137
  107.5 9.9 %all-to-all-done.1 = bf16[4,64,1024]{2,1,0:T(8,128)(2,1)S(1)} async-done(((bf16[4,64,1024]{2,1,0:T(8,128)(2,1)}), bf16[4,64,1024]{2,1,0:T(8,128)(2,1)S(1)}, u32[]{:S(2)}, u32[]{:S(2)}) %all-to-all-start.1) | async-done | bytes 524320 | tf_op jit(solution)/shard_map/all_to_all | solution.py:76
  117.4 3.5 %all-to-all-start.3 = ((bf16[4,64,1024]{2,1,0:T(8,128)(2,1)}), bf16[4,64,1024]{2,1,0:T(8,128)(2,1)S(1)}, u32[]{:S(2)}, u32[]{:S(2)}) async-start(bf16[4,64,1024]{2,1,0:T(8,128)(2,1)} %convert_element_type.137), calls=%async_computation.3 | async-start | bytes 1048576 | tf_op jit(solution)/shard_map/all_to_all | solution.py:89
  120.9 0.1 collective-permute-start.1
  121.0 0.1 convert_bitcast_fusion
  121.1 1.1 copy.113
  122.2 8.9 %all-to-all-done.3 = bf16[4,64,1024]{2,1,0:T(8,128)(2,1)S(1)} async-done(((bf16[4,64,1024]{2,1,0:T(8,128)(2,1)}), bf16[4,64,1024]{2,1,0:T(8,128)(2,1)S(1)}, u32[]{:S(2)}, u32[]{:S(2)}) %all-to-all-start.3) | async-done | bytes 524320 | tf_op jit(solution)/shard_map/all_to_all | solution.py:89
  131.2 0.1 convert_bitcast_fusion.1
  131.3 0.1 copy.114
  131.4 0.2 fusion.24
  131.6 0.2 fusion.23
  131.8 1.4 fusion.22
  133.3 2.2 %fusion.19 = (bf16[64,4096]{1,0:T(8,128)(2,1)S(1)}, bf16[64,4096]{1,0:T(8,128)(2,1)}) fusion(bf16[64,4096]{1,0:T(8,128)(2,1)} %collective-permute-done.1, f32[64,4096]{1,0:T(8,128)S(1)} %bitcast.152, f32[64]{0:T(128)S(1)} %broadcast_multiply_fusion, f32[64]{0:T(128)S(1)} %get-tuple-element.51, f32[64]{0:T(128)S(1)} %get-tuple-element.52, ...), kind=kLoop, calls=%fused_computation.38 | loop fusion | flops 2621440 | bytes 3687424 | tf_op jit(solution)/shard_map/convert_element_type | solution.py:96
  135.5 0.8 copy.137
  136.3 3.5 %all-to-all-start.4 = ((bf16[64,4,1024]{2,0,1:T(8,128)(2,1)}), bf16[64,4,1024]{2,0,1:T(8,128)(2,1)S(1)}, u32[]{:S(2)}, u32[]{:S(2)}) async-start(bf16[64,4,1024]{2,0,1:T(8,128)(2,1)} %bitcast.161), calls=%async_computation.4 | async-start | bytes 1048576 | tf_op jit(solution)/shard_map/all_to_all | solution.py:100
  139.8 0.7 iota_compare_fusion
  140.5 9.6 %all-to-all-done.4 = bf16[64,4,1024]{2,0,1:T(8,128)(2,1)S(1)} async-done(((bf16[64,4,1024]{2,0,1:T(8,128)(2,1)}), bf16[64,4,1024]{2,0,1:T(8,128)(2,1)S(1)}, u32[]{:S(2)}, u32[]{:S(2)}) %all-to-all-start.4) | async-done | bytes 524320 | tf_op jit(solution)/shard_map/all_to_all | solution.py:100
  150.1 0.8 copy-done.3
  150.9 1.1 copy.117
  152.0 1.1 copy.90
  153.1 1.2 multiply_reduce_fusion
  154.3 3.5 %fusion.38 = (bf16[256,8,256]{2,0,1:T(8,128)(2,1)}, bf16[256,8,256]{2,0,1:T(8,128)(2,1)S(1)}, f32[256,256,8]{1,0,2:T(8,128)}) fusion(f32[8,256]{1,0:T(8,128)S(1)} %fusion.12, f32[8,256]{1,0:T(8,128)S(1)} %get-tuple-element.53, f32[256,256,8]{1,0,2:T(8,128)S(1)} %get-tuple-element.54, pred[256,256]{1,0:T(8,128)(4,1)} %iota_compare_fusion, ...), kind=kOutput, calls=%fused_computation.59 | convolution fusion | flops 138936320 | bytes 6971396 | tf_op jit(solution)/shard_map/ihd,jd->hij/dot_general | solution.py:116
  157.9 1.1 convolution_bitcast_fusion.1
  158.9 3.3 %all-to-all-start.6 = ((bf16[4,64,128]{2,1,0:T(8,128)(2,1)}), bf16[4,64,128]{2,1,0:T(8,128)(2,1)S(1)}, u32[]{:S(2)}, u32[]{:S(2)}) async-start(bf16[4,64,128]{2,1,0:T(8,128)(2,1)} %convolution_bitcast_fusion.1), calls=%async_computation.6 | async-start | bytes 131072 | tf_op jit(solution)/shard_map/all_to_all | solution.py:139
  162.2 2.3 %convolution_bitcast_fusion = bf16[4,64,128]{2,1,0:T(8,128)(2,1)} fusion(bf16[4,64,8,256]{3,1,0,2:T(8,128)(2,1)} %bitcast.174, bf16[256,8,128,1]{2,1,0,3:T(8,128)(2,1)S(1)} %bitcast.159), kind=kOutput, calls=%fused_computation.35 | convolution fusion | flops 134217728 | bytes 1638400 | tf_op jit(solution)/shard_map/hij,ihd->jd/dot_general | solution.py:114
  164.5 3.4 %all-to-all-done.6 = bf16[4,64,128]{2,1,0:T(8,128)(2,1)S(1)} async-done(((bf16[4,64,128]{2,1,0:T(8,128)(2,1)}), bf16[4,64,128]{2,1,0:T(8,128)(2,1)S(1)}, u32[]{:S(2)}, u32[]{:S(2)}) %all-to-all-start.6) | async-done | bytes 65568 | tf_op jit(solution)/shard_map/all_to_all | solution.py:139
  167.9 3.3 %all-to-all-start.7 = ((bf16[4,64,128]{2,1,0:T(8,128)(2,1)}), bf16[4,64,128]{2,1,0:T(8,128)(2,1)S(1)}, u32[]{:S(2)}, u32[]{:S(2)}) async-start(bf16[4,64,128]{2,1,0:T(8,128)(2,1)} %convolution_bitcast_fusion), calls=%async_computation.7 | async-start | bytes 131072 | tf_op jit(solution)/shard_map/all_to_all | solution.py:140
  171.2 2.5 %fusion.17 = bf16[256,8,128]{0,2,1:T(8,128)(2,1)S(1)} fusion(f32[256,256,8]{1,0,2:T(8,128)} %get-tuple-element.57, f32[8,256]{1,0:T(8,128)S(1)} %bitcast.172, f32[256,256,8]{1,0,2:T(8,128)S(1)} %get-tuple-element.54, f32[8,256]{1,0:T(8,128)S(1)} %fusion.12, f32[8,256]{1,0:T(8,128)S(1)} %get-tuple-element.53, pred[256,256]{0,1:T(8,128)(4,1)S(1)} %iota_compare_fusion.1, ...), kind=kOutput, calls=%fused_computation.34 | convolution fusion | flops 138674176 | bytes 4874244 | tf_op jit(solution)/shard_map/hij,jd->ihd/dot_general | solution.py:125
  173.8 0.3 copy.93
  174.1 1.0 convert_element_type.148
  175.1 2.1 all-to-all-done.7
  177.2 4.6 %all-to-all-start.5 = ((bf16[4,64,1024]{2,1,0:T(8,128)(2,1)}), bf16[4,64,1024]{2,1,0:T(8,128)(2,1)S(1)}, u32[]{:S(2)}, u32[]{:S(2)}) async-start(bf16[4,64,1024]{2,1,0:T(8,128)(2,1)} %convert_element_type.148), calls=%async_computation.5 | async-start | bytes 1048576 | tf_op jit(solution)/shard_map/all_to_all | solution.py:137
  181.9 0.6 dynamic-slice.14
  183.1 19.2 %all-reduce = f32[4096]{0:T(1024)S(1)} all-reduce(f32[4096]{0:T(1024)S(1)} %get-tuple-element.45), channel_id=6, replica_groups=mesh['dp'=4,'pipe'=2,'seq'=4] {'seq'}, use_global_device_ids=true, to_apply=%region_9.10.clone | all-reduce | flops 4096 | bytes 32768
  202.3 10.5 %psum.7 = f32[1,1024]{1,0:T(1,128)} all-reduce(f32[1,1024]{1,0:T(1,128)S(1)} %bitcast.170), channel_id=1, replica_groups=mesh['dp'=4,'pipe'=2,'seq'=4] {'dp'}, use_global_device_ids=true, to_apply=%region_10.11 | all-reduce | flops 1024 | bytes 8192 | tf_op jit(solution)/shard_map/psum | solution.py:99
  212.8 0.1 copy.96
  212.9 0.7 convert_element_type.152
  213.5 0.1 copy.98
  213.6 0.7 convert_element_type.156
  214.3 0.4 copy.94
  214.7 1.2 broadcast_in_dim.61
  215.8 0.8 copy.139
  (38 shorter events, 0.1 us)
Async XLA Ops:
  0.6 8.9 %copy-start.7 = (bf16[1,1,64,4096]{3,2,1,0:T(8,128)(2,1)S(1)}, bf16[1,1,64,4096]{3,2,1,0:T(8,128)(2,1)}, u32[]{:S(2)}) copy-start(bf16[1,1,64,4096]{3,2,1,0:T(8,128)(2,1)} %param.19) | copy-start | bytes 1572868
  3.1 24.4 %copy-start.8 = (bf16[1,1,64,512]{3,2,1,0:T(8,128)(2,1)S(1)}, bf16[1,1,64,512]{3,2,1,0:T(8,128)(2,1)}, u32[]{:S(2)}) copy-start(bf16[1,1,64,512]{3,2,1,0:T(8,128)(2,1)} %param.20) | copy-start | bytes 196612
  3.1 46.0 %copy-start.9 = (bf16[1,1,64,512]{3,2,1,0:T(8,128)(2,1)S(1)}, bf16[1,1,64,512]{3,2,1,0:T(8,128)(2,1)}, u32[]{:S(2)}) copy-start(bf16[1,1,64,512]{3,2,1,0:T(8,128)(2,1)} %param.21) | copy-start | bytes 196612
  3.1 20.9 %all-to-all-start = ((bf16[64,4,1024]{2,0,1:T(8,128)(2,1)}), bf16[64,4,1024]{2,0,1:T(8,128)(2,1)S(1)}, u32[]{:S(2)}, u32[]{:S(2)}) async-start(bf16[64,4,1024]{2,0,1:T(8,128)(2,1)} %copy.76), calls=%async_computation | async-start | bytes 1048576 | tf_op jit(solution)/shard_map/all_to_all | solution.py:35
  9.5 54.5 %copy-start.10 = (bf16[1,1,64,512]{3,2,1,0:T(8,128)(2,1)S(1)}, bf16[1,1,64,512]{3,2,1,0:T(8,128)(2,1)}, u32[]{:S(2)}) copy-start(bf16[1,1,64,512]{3,2,1,0:T(8,128)(2,1)} %param.17) | copy-start | bytes 196612
  9.5 68.4 %copy-start.11 = (bf16[1,1,64,512]{3,2,1,0:T(8,128)(2,1)S(1)}, bf16[1,1,64,512]{3,2,1,0:T(8,128)(2,1)}, u32[]{:S(2)}) copy-start(bf16[1,1,64,512]{3,2,1,0:T(8,128)(2,1)} %param.18) | copy-start | bytes 196612
  24.0 68.0 %all-to-all-start.2 = ((bf16[64,4,1024]{2,0,1:T(8,128)(2,1)}), bf16[64,4,1024]{2,0,1:T(8,128)(2,1)S(1)}, u32[]{:S(2)}, u32[]{:S(2)}) async-start(bf16[64,4,1024]{2,0,1:T(8,128)(2,1)} %copy.81), calls=%async_computation.2 | async-start | bytes 1048576 | tf_op jit(solution)/shard_map/all_to_all | solution.py:35
  92.1 9.8 %copy-start.4 = (bf16[32,8,8,128]{3,2,1,0:T(8,128)(2,1)}, bf16[32,8,8,128]{3,2,1,0:T(8,128)(2,1)S(1)}, u32[]{:S(2)}) copy-start(bf16[32,8,8,128]{3,2,1,0:T(8,128)(2,1)S(1)} %copy.116) | copy-start | bytes 1572868
  97.5 19.9 %all-to-all-start.1 = ((bf16[4,64,1024]{2,1,0:T(8,128)(2,1)}), bf16[4,64,1024]{2,1,0:T(8,128)(2,1)S(1)}, u32[]{:S(2)}, u32[]{:S(2)}) async-start(bf16[4,64,1024]{2,1,0:T(8,128)(2,1)} %convert_element_type.127), calls=%async_computation.1 | async-start | bytes 1048576 | tf_op jit(solution)/shard_map/all_to_all | solution.py:76
  104.4 13.1 %copy-start.1 = (bf16[256,8,128]{0,2,1:T(8,128)(2,1)}, bf16[256,8,128]{0,2,1:T(8,128)(2,1)S(1)}, u32[]{:S(2)}) copy-start(bf16[256,8,128]{0,2,1:T(8,128)(2,1)S(1)} %fusion.16) | copy-start | bytes 1572868
  104.4 16.6 %copy-start.12 = (bf16[1,4096]{1,0:T(2,128)(2,1)S(1)}, bf16[1,4096]{1,0:T(2,128)(2,1)}, u32[]{:S(2)}) copy-start(bf16[1,4096]{1,0:T(2,128)(2,1)} %param.23) | copy-start | bytes 24580
  117.4 13.7 %all-to-all-start.3 = ((bf16[4,64,1024]{2,1,0:T(8,128)(2,1)}), bf16[4,64,1024]{2,1,0:T(8,128)(2,1)S(1)}, u32[]{:S(2)}, u32[]{:S(2)}) async-start(bf16[4,64,1024]{2,1,0:T(8,128)(2,1)} %convert_element_type.137), calls=%async_computation.3 | async-start | bytes 1048576 | tf_op jit(solution)/shard_map/all_to_all | solution.py:89
  120.9 10.9 %collective-permute-start.1 = (bf16[64,4096]{1,0:T(8,128)(2,1)}, bf16[64,4096]{1,0:T(8,128)(2,1)}, u32[]{:S(2)}, u32[]{:S(2)}) collective-permute-start(bf16[64,4096]{1,0:T(8,128)(2,1)} %bitcast.173), channel_id=1, source_target_pairs={{0,4},{4,0},{1,5},{5,1},{2,6},{6,2},{3,7},{7,3},{8,12},{12,8},{9,1... | collective-permute-start | bytes 1572872 | tf_op jit(solution)/shard_map/ppermute | solution.py:19
  131.3 2.0 copy-start
  135.5 17.6 %copy-start.2 = (bf16[256,8,128]{0,2,1:T(8,128)(2,1)S(1)}, bf16[256,8,128]{0,2,1:T(8,128)(2,1)}, u32[]{:S(2)}) copy-start(bf16[256,8,128]{0,2,1:T(8,128)(2,1)} %copy-done.1) | copy-start | bytes 1572868
  136.3 13.7 %all-to-all-start.4 = ((bf16[64,4,1024]{2,0,1:T(8,128)(2,1)}), bf16[64,4,1024]{2,0,1:T(8,128)(2,1)S(1)}, u32[]{:S(2)}, u32[]{:S(2)}) async-start(bf16[64,4,1024]{2,0,1:T(8,128)(2,1)} %bitcast.161), calls=%async_computation.4 | async-start | bytes 1048576 | tf_op jit(solution)/shard_map/all_to_all | solution.py:100
  150.1 0.8 copy-start.3
  154.3 3.6 %copy-start.5 = (bf16[32,8,8,128]{3,2,1,0:T(8,128)(2,1)S(1)}, bf16[32,8,8,128]{3,2,1,0:T(8,128)(2,1)}, u32[]{:S(2)}) copy-start(bf16[32,8,8,128]{3,2,1,0:T(8,128)(2,1)} %copy-done.4) | copy-start | bytes 1572868
  158.9 9.0 %all-to-all-start.6 = ((bf16[4,64,128]{2,1,0:T(8,128)(2,1)}), bf16[4,64,128]{2,1,0:T(8,128)(2,1)S(1)}, u32[]{:S(2)}, u32[]{:S(2)}) async-start(bf16[4,64,128]{2,1,0:T(8,128)(2,1)} %convolution_bitcast_fusion.1), calls=%async_computation.6 | async-start | bytes 131072 | tf_op jit(solution)/shard_map/all_to_all | solution.py:139
  167.9 9.3 %all-to-all-start.7 = ((bf16[4,64,128]{2,1,0:T(8,128)(2,1)}), bf16[4,64,128]{2,1,0:T(8,128)(2,1)S(1)}, u32[]{:S(2)}, u32[]{:S(2)}) async-start(bf16[4,64,128]{2,1,0:T(8,128)(2,1)} %convolution_bitcast_fusion), calls=%async_computation.7 | async-start | bytes 131072 | tf_op jit(solution)/shard_map/all_to_all | solution.py:140
  173.8 8.1 %copy-start.6 = (bf16[64,4096]{1,0:T(8,128)(2,1)S(1)}, bf16[64,4096]{1,0:T(8,128)(2,1)}, u32[]{:S(2)}) copy-start(bf16[64,4096]{1,0:T(8,128)(2,1)} %get-tuple-element.50) | copy-start | bytes 1572868
  173.8 8.1 %copy-start.13 = (u32[32]{0:T(128)S(1)}, u32[32]{0:T(128)}, u32[]{:S(2)}) copy-start(u32[32]{0:T(128)} %constant.119) | copy-start | bytes 388
  177.2 37.0 %all-to-all-start.5 = ((bf16[4,64,1024]{2,1,0:T(8,128)(2,1)}), bf16[4,64,1024]{2,1,0:T(8,128)(2,1)S(1)}, u32[]{:S(2)}, u32[]{:S(2)}) async-start(bf16[4,64,1024]{2,1,0:T(8,128)(2,1)} %convert_element_type.148), calls=%async_computation.5 | async-start | bytes 1048576 | tf_op jit(solution)/shard_map/all_to_all | solution.py:137
  181.8 31.0 %collective-permute-start = (bf16[64,4096]{1,0:T(8,128)(2,1)S(1)}, bf16[64,4096]{1,0:T(8,128)(2,1)S(1)}, u32[]{:S(2)}, u32[]{:S(2)}) collective-permute-start(bf16[64,4096]{1,0:T(8,128)(2,1)S(1)} %copy-done.6), channel_id=1, source_target_pairs={{0,4},{4,0},{1,5},{5,1},{2,6},{6,2},{3,7},{7,3},{8,12},{12,8},{9,1... | collective-permute-start | bytes 1572872 | tf_op jit(solution)/shard_map/ppermute | solution.py:19
where the time goes:
time: 218 us; the launch traced here: 217 us
  blocking collectives  94 us (43%)
  waiting for transfers between devices  47.1 us (22%)
  starting transfers between devices  32.5 us (15%)
  local copies, waits for them, and re-layouts  19.2 us (9%)
  matrix products  15.5 us (7%)
  other arithmetic  6.64 us (3%)
    all_gather x2, blocking collectives, heads_layout(): lax.all_gather(keys, 'seq', axis=0, tiled=True)  35.5 us
    all_gather x2, blocking collectives, heads_layout(): lax.all_gather(values, 'seq', axis=0, tiled=True)  28.9 us
    unnamed x1, blocking collectives  19.2 us
    all_to_all x2, waiting for transfers between devices, heads_layout(): lax.all_to_all(query, 'seq', split_axis=1, concat_axis=0, tiled=True)  13.1 us
    psum x1, blocking collectives, local(): grad_gain = lax.psum(gain_share, 'dp')  10.5 us
    all_to_all x2, starting transfers between devices, heads_layout(): lax.all_to_all(query, 'seq', split_axis=1, concat_axis=0, tiled=True)  9.92 us
    all_to_all x1, waiting for transfers between devices, local(): lax.all_to_all(first_out, 'seq', split_axis=0, concat_axis=1, tiled=True)  9.89 us
    all_to_all x1, waiting for transfers between devices, local(): lax.all_to_all(grad_tokens, 'seq', split_axis=1, concat_axis=0, tiled=True)  9.6 us
  transfers between devices with their start and end apart: 10, of which 6 were waited for; matrix products, arithmetic and copies ran while one was open for 8% of the time, Pallas kernels for 0%

commit v1 on v0

v1 whole, which is shorter than its diff:
```python
import functools
import math

import jax
import jax.numpy as jnp
from jax import lax
from jax.experimental import pallas as pl
from jax.experimental.pallas import tpu as pltpu
from jax.sharding import PartitionSpec as P

QH = 32
KVH = 4
HD = 128
HPG = QH // KVH
WIDTH = QH * HD
EPS = 1e-05
SCALE = 1.0 / math.sqrt(HD)
SCALE_LOG2 = SCALE * math.log2(math.e)
MESH = pl.DeviceIdType.MESH
F32 = jnp.float32
BF16 = jnp.bfloat16


def head(h):
    return slice(h * HD, (h + 1) * HD)


def dot(a, b, contract):
    return lax.dot_general(a, b, ((contract[:1], contract[1:]), ((), ())), preferred_element_type=F32)


def kernel(
    n, pipes, replicas, rows,
    q1_in, k1_in, v1_in, q2_in, k2_in, v2_in, go_in, gain_ref,
    next_out, gq_out, gk_out, gv_out, gain_out,
    q1, q2, up, k1, v1, k2, v2, probs, o1, o2, grad, gq, part, own, land,
    gpart, gland, gshare,
    local_sem, kv_send, kv_recv, part_send, part_recv, out_sem,
    pipe_send, pipe_recv, gain_send, gain_recv, rep_send, rep_recv,
):
    me = lax.axis_index("seq")
    section = lax.axis_index("pipe")
    replica = lax.axis_index("dp")
    length = n * rows
    behind = lax.rem(section + pipes - 1, pipes)
    ahead = lax.rem(section + 1, pipes)

    def block(b):
        return pl.ds(pl.multiple_of(b * rows, rows), rows)

    locals_ = [
        pltpu.make_async_copy(src, dst, local_sem.at[i])
        for i, (src, dst) in enumerate(
            (
                (q2_in, q2),
                (k2_in, k2.at[block(me)]),
                (v2_in, v2.at[block(me)]),
                (q1_in, q1),
                (k1_in, k1.at[block(me)]),
                (v1_in, v1.at[block(me)]),
            )
        )
    ]
    for copy in locals_:
        copy.start()

    barrier = pltpu.get_barrier_semaphore()
    for d in range(1, n):
        pl.semaphore_signal(barrier, inc=1, device_id={"seq": lax.rem(me + d, n)}, device_id_type=MESH)
    for d in range(1, replicas):
        pl.semaphore_signal(
            barrier, inc=1, device_id={"dp": lax.rem(replica + d, replicas)}, device_id_type=MESH
        )
    for other in (behind, ahead):
        pl.semaphore_signal(barrier, inc=1, device_id={"pipe": other}, device_id_type=MESH)

    for b in range(1, n):

        @pl.when(b > me)
        def _():
            for ref in (k1, v1, k2, v2):
                ref[b * rows : (b + 1) * rows, :] = jnp.zeros((rows, KVH * HD), BF16)

    pl.semaphore_wait(barrier, n - 1 + replicas - 1 + 2)

    def kv_copy(array, g, d, source):
        src = (k2_in, v2_in, k1_in, v1_in)[array]
        dst = (k2, v2, k1, v1)[array]
        return pltpu.make_async_remote_copy(
            src_ref=src.at[:, head(g)],
            dst_ref=dst.at[block(source), head(g)],
            send_sem=kv_send.at[array, g, d - 1],
            recv_sem=kv_recv.at[array, g, d - 1],
            device_id={"seq": lax.rem(me + d, n)},
            device_id_type=MESH,
        )

    def kv_start(arrays, g):
        for d in range(n - 1, 0, -1):

            @pl.when(me + d < n)
            def _():
                for array in arrays:
                    kv_copy(array, g, d, me).start()

    def kv_wait(arrays, g):
        for d in range(1, n):

            @pl.when(me >= d)
            def _():
                for array in arrays:
                    kv_copy(array, g, d, me - d).wait_recv()

    for g in range(KVH):
        kv_start((0, 1), g)
    upstream = pltpu.make_async_remote_copy(
        src_ref=go_in, dst_ref=up, send_sem=pipe_send.at[0], recv_sem=pipe_recv.at[0],
        device_id={"pipe": behind}, device_id_type=MESH,
    )
    upstream.start()
    for g in range(KVH):
        kv_start((2, 3), g)

    token = me * rows + lax.broadcasted_iota(jnp.int32, (rows, length), 0)
    allowed = (lax.broadcasted_iota(jnp.int32, (rows, length), 1) <= token)[None]

    def stack(ref, g):
        return jnp.concatenate([ref[:, head(g * HPG + h)] for h in range(HPG)], axis=0)

    def forward(q, k, v, o, g):
        scores = dot(stack(q, g), k[:, head(g)], (1, 1)).reshape(HPG, rows, length)
        scores = jnp.where(allowed, scores, -jnp.inf)
        highest = jnp.max(scores, axis=-1, keepdims=True)
        exponent = jnp.exp2((scores - highest) * SCALE_LOG2)
        prob = exponent * (1.0 / jnp.sum(exponent, axis=-1, keepdims=True))
        prob = prob.reshape(HPG * rows, length)
        out = dot(prob.astype(BF16), v[:, head(g)], (1, 0)).astype(BF16)
        squares = jnp.zeros((rows, HD), F32)
        for h in range(HPG):
            piece = out[h * rows : (h + 1) * rows]
            o[:, head(g * HPG + h)] = piece
            squares += piece.astype(F32) * piece.astype(F32)
        return prob, squares

    def inverse_of(squares):
        return lax.rsqrt(jnp.sum(squares, axis=-1, keepdims=True) * (1.0 / WIDTH) + EPS)

    for copy in locals_[:3]:
        copy.wait()
    squares = jnp.zeros((rows, HD), F32)
    for g in range(KVH):
        kv_wait((0, 1), g)
        prob, more = forward(q2, k2, v2, o2, g)
        probs[g] = prob
        squares += more
    inverse = inverse_of(squares)

    upstream.wait_recv()
    cross = jnp.zeros((rows, HD), F32)
    share = QH // n
    for h in range(QH):
        activity = o2[:, head(h)].astype(F32)
        product = up[:, head(h)].astype(F32) * activity
        cross += gain_ref[:, head(h)].astype(F32) * product
        gpart[h // share, h % share : h % share + 1, :] = jnp.sum(product * inverse, axis=0, keepdims=True)
    cross_mean = jnp.sum(cross, axis=-1, keepdims=True) * (1.0 / WIDTH)
    factor = inverse * inverse * inverse * cross_mean
    for h in range(QH):
        gained = gain_ref[:, head(h)].astype(F32) * up[:, head(h)].astype(F32)
        grad[:, head(h)] = (gained * inverse - o2[:, head(h)].astype(F32) * factor).astype(BF16)

    def gain_copy(d):
        owner = lax.rem(me + d, n)
        return pltpu.make_async_remote_copy(
            src_ref=gpart.at[owner], dst_ref=gland.at[d - 1],
            send_sem=gain_send.at[d - 1], recv_sem=gain_recv.at[d - 1],
            device_id={"seq": owner}, device_id_type=MESH,
        )

    for d in range(1, n):
        gain_copy(d).start()

    def part_copy(g, d, target):
        return pltpu.make_async_remote_copy(
            src_ref=part.at[target, g], dst_ref=land.at[d - 1, g],
            send_sem=part_send.at[g, d - 1], recv_sem=part_recv.at[g, d - 1],
            device_id={"seq": target}, device_id_type=MESH,
        )

    def gq_copy(g):
        lanes = slice(g * HPG * HD, (g + 1) * HPG * HD)
        return pltpu.make_async_copy(gq.at[:, lanes], gq_out.at[:, lanes], out_sem.at[g])

    for g in range(KVH):
        grads = stack(grad, g)
        outs = stack(o2, g)
        prob = probs[g]
        dots = jnp.sum(grads.astype(F32) * outs.astype(F32), axis=-1, keepdims=True)
        grad_weights = dot(grads, v2[:, head(g)], (1, 1))
        grad_scores = (prob * (grad_weights - dots) * SCALE).astype(BF16)
        for which, value in enumerate(
            (dot(grad_scores, stack(q2, g), (0, 0)), dot(prob.astype(BF16), grads, (0, 0)))
        ):
            own[g, which] = value
            for b in range(n - 1):
                part[b, g, which] = value[b * rows : (b + 1) * rows].astype(BF16)
        for d in range(n - 1, 0, -1):

            @pl.when(me >= d)
            def _():
                part_copy(g, d, me - d).start()

        grad_query = dot(grad_scores, k2[:, head(g)], (1, 0)).astype(BF16)
        for h in range(HPG):
            gq[:, head(g * HPG + h)] = grad_query[h * rows : (h + 1) * rows]
        gq_copy(g).start()

    for d in range(1, n):
        gain_copy(d).wait_recv()
    total = gpart[me]
    for d in range(1, n):
        total += gland[d - 1]
    gshare[replica] = total

    def replica_copy(d, source):
        return pltpu.make_async_remote_copy(
            src_ref=gshare.at[source], dst_ref=gshare.at[source],
            send_sem=rep_send.at[d - 1], recv_sem=rep_recv.at[d - 1],
            device_id={"dp": lax.rem(replica + d, replicas)}, device_id_type=MESH,
        )

    for d in range(1, replicas):
        replica_copy(d, replica).start()

    for copy in locals_[3:]:
        copy.wait()
    squares = jnp.zeros((rows, HD), F32)
    for g in range(KVH):
        kv_wait((2, 3), g)
        prob, more = forward(q1, k1, v1, o1, g)
        squares += more
    inverse = inverse_of(squares)
    for h in range(QH):
        gain = gain_ref[:, head(h)].astype(F32)
        o1[:, head(h)] = (gain * o1[:, head(h)].astype(F32) * inverse).astype(BF16)
    normed = pltpu.make_async_remote_copy(
        src_ref=o1, dst_ref=next_out, send_sem=pipe_send.at[1], recv_sem=pipe_recv.at[1],
        device_id={"pipe": ahead}, device_id_type=MESH,
    )
    normed.start()

    for g in range(KVH):
        for d in range(1, n):

            @pl.when(me + d < n)
            def _():
                part_copy(g, d, me).wait_recv()
                for which in range(2):
                    own[g, which, block(me), :] += land[d - 1, g, which].astype(F32)

        gk_out[:, head(g)] = own[g, 0, block(me), :].astype(BF16)
        gv_out[:, head(g)] = own[g, 1, block(me), :].astype(BF16)

    for d in range(1, replicas):
        replica_copy(d, lax.rem(replica + replicas - d, replicas)).wait_recv()
    total = gshare[0]
    for r in range(1, replicas):
        total += gshare[r]
    for h in range(share):
        gain_out[:, head(h)] = total[h : h + 1]

    for d in range(1, n):

        @pl.when(me + d < n)
        def _():
            for g in range(KVH):
                for array in range(4):
                    kv_copy(array, g, d, me).wait_send()

        @pl.when(me >= d)
        def _():
            for g in range(KVH):
                part_copy(g, d, me - d).wait_send()

        gain_copy(d).wait_send()
    for d in range(1, replicas):
        replica_copy(d, replica).wait_send()
    upstream.wait_send()
    for g in range(KVH):
        gq_copy(g).wait()
    normed.wait()


def local(n, pipes, replicas, q1, k1, v1, q2, k2, v2, go, gain):
    rows = q1.shape[2]
    length = n * rows
    share = QH // n
    args = [x[0, 0] for x in (q1, k1, v1, q2, k2, v2, go)] + [gain]
    anywhere = pl.BlockSpec(memory_space=pl.ANY)
    vmem = pl.BlockSpec(memory_space=pltpu.VMEM)
    wide = pltpu.VMEM((rows, WIDTH), BF16)
    keys = pltpu.VMEM((length, KVH * HD), BF16)
    dma = pltpu.SemaphoreType.DMA
    flops = 2 * 7 * rows * length * HD * QH
    outs = pl.pallas_call(
        functools.partial(kernel, n, pipes, replicas, rows),
        out_shape=(
            jax.ShapeDtypeStruct((rows, WIDTH), BF16),
            jax.ShapeDtypeStruct((rows, WIDTH), BF16),
            jax.ShapeDtypeStruct((rows, KVH * HD), BF16),
            jax.ShapeDtypeStruct((rows, KVH * HD), BF16),
            jax.ShapeDtypeStruct((1, WIDTH // n), F32),
        ),
        in_specs=[anywhere] * 7 + [vmem],
        out_specs=(anywhere, anywhere, vmem, vmem, vmem),
        scratch_shapes=[
            wide, wide, wide, keys, keys, keys, keys,
            pltpu.VMEM((KVH, HPG * rows, length), F32),
            wide, wide, wide, wide,
            pltpu.VMEM((n, KVH, 2, rows, HD), BF16),
            pltpu.VMEM((KVH, 2, length, HD), F32),
            pltpu.VMEM((n - 1, KVH, 2, rows, HD), BF16),
            pltpu.VMEM((n, share, HD), F32),
            pltpu.VMEM((n - 1, share, HD), F32),
            pltpu.VMEM((replicas, share, HD), F32),
            dma((6,)),
            dma((4, KVH, n - 1)), dma((4, KVH, n - 1)),
            dma((KVH, n - 1)), dma((KVH, n - 1)),
            dma((KVH,)),
            dma((2,)), dma((2,)),
            dma((n - 1,)), dma((n - 1,)),
            dma((replicas - 1,)), dma((replicas - 1,)),
        ],
        compiler_params=pltpu.CompilerParams(
            collective_id=0, has_side_effects=True, vmem_limit_bytes=48 * 1024 * 1024
        ),
        cost_estimate=pl.CostEstimate(flops=flops, bytes_accessed=8 * rows * WIDTH, transcendentals=0),
    )(*args)
    nxt, gq, gk, gv, gg = outs
    return nxt[None, None], gq[None, None], gk[None, None], gv[None, None], gg


def solution(mesh):
    tokens = P("dp", "pipe", "seq", None)
    sizes = (mesh.shape["seq"], mesh.shape["pipe"], mesh.shape["dp"])
    return jax.shard_map(
        functools.partial(local, *sizes),
        mesh=mesh,
        in_specs=(tokens,) * 7 + (P("pipe", None),),
        out_specs=(tokens,) * 4 + (P("pipe", "seq"),),
        check_vma=False,
    )
```

time: 218 us -> 47.3 us (0.22)
  blocking collectives: 94 us -> 0 us
  waiting for transfers between devices: 47.1 us -> 0 us
  Pallas kernels: 0 us -> 35.5 us
  starting transfers between devices: 32.5 us -> 0 us
  matrix products: 15.5 us -> 0 us
  local copies, waits for them, and re-layouts: 19.2 us -> 10.6 us
  other arithmetic: 6.64 us -> 0 us
    all_gather x4 -> x0, blocking collectives: 64.3 us -> none  [the longest x2 35.5 us: heads_layout(): lax.all_gather(keys, 'seq', axis=0, tiled=True)]
    all_to_all x8 -> x0, waiting for transfers between devices: 47.1 us -> none  [the longest x2 13.1 us: heads_layout(): lax.all_to_all(query, 'seq', split_axis=1, concat_axis=0, tiled=True)]
    pallas_call x0 -> x1, Pallas kernels: none -> 35.5 us  [local(): pl.pallas_call(functools.partial(kernel, n, pipes, replicas, rows), out_s...]
    all_to_all x8 -> x0, starting transfers between devices: 32.4 us -> none  [the longest x2 9.92 us: heads_layout(): lax.all_to_all(query, 'seq', split_axis=1, concat_axis=0, tiled=True)]
    unnamed x1 -> x0, blocking collectives: 19.2 us -> none
    dot_general x7 -> x0, matrix products: 13.4 us -> none  [the longest x1 3.55 us: local(): jnp.einsum('ihd,jd->hij', grad_block, second_values[:finish], preferred_e...]
    psum x1 -> x0, blocking collectives: 10.5 us -> none  [local(): grad_gain = lax.psum(gain_share, 'dp')]
    convert_element_type x12 -> x0, local copies, waits for them, and re-layouts: 8.38 us -> none  [the longest x4 4.46 us: causal_forward(): outputs.append(result.reshape(block_rows, head_width).astype(jnp.bfloat16))]
  transfers between devices with their start and end apart: 10 -> 0, of which waited for: 6 -> 0; matrix products, arithmetic and copies ran while one was open for 8% -> 0% of each run, Pallas kernels for 0% -> 0%
where the time goes in v1:
time: 47.3 us; the launch traced here: 46.8 us
  Pallas kernels  35.5 us (75%)
  local copies, waits for them, and re-layouts  10.6 us (22%)
  between operations  0.66 us (1%)
    pallas_call x1, Pallas kernels, local(): pl.pallas_call(functools.partial(kernel, n, pipes, replicas, rows), out_s...  35.5 us
    unnamed x21, local copies, waits for them, and re-layouts  10.6 us

profile of v1, /device:TPU:0, one launch (start us, length us, event | category | flops | bytes accessed | tf_op | source)
XLA Modules:
  0.0 46.8 jit_solution(1478932696544769295)
XLA Ops:
  0.6 0.0 copy-start
  0.6 1.0 %copy-done = bf16[1,1,64,4096]{3,2,1,0:T(8,128)(2,1)S(1)} copy-done((bf16[1,1,64,4096]{3,2,1,0:T(8,128)(2,1)S(1)}, bf16[1,1,64,4096]{3,2,1,0:T(8,128)(2,1)}, u32[]{:S(2)}) %copy-start) | copy-done | bytes 524312
  1.7 0.0 copy-start.1
  1.7 1.0 %copy-done.1 = bf16[1,1,64,4096]{3,2,1,0:T(8,128)(2,1)S(1)} copy-done((bf16[1,1,64,4096]{3,2,1,0:T(8,128)(2,1)S(1)}, bf16[1,1,64,4096]{3,2,1,0:T(8,128)(2,1)}, u32[]{:S(2)}) %copy-start.1) | copy-done | bytes 524312
  2.7 0.0 copy-start.2
  2.7 1.0 %copy-done.2 = bf16[1,1,64,4096]{3,2,1,0:T(8,128)(2,1)S(1)} copy-done((bf16[1,1,64,4096]{3,2,1,0:T(8,128)(2,1)S(1)}, bf16[1,1,64,4096]{3,2,1,0:T(8,128)(2,1)}, u32[]{:S(2)}) %copy-start.2) | copy-done | bytes 524312
  3.8 0.0 copy-start.3
  3.8 0.8 %copy-done.3 = bf16[1,1,64,512]{3,2,1,0:T(8,128)(2,1)S(1)} copy-done((bf16[1,1,64,512]{3,2,1,0:T(8,128)(2,1)S(1)}, bf16[1,1,64,512]{3,2,1,0:T(8,128)(2,1)}, u32[]{:S(2)}) %copy-start.3) | copy-done | bytes 65560
  4.6 0.0 copy-start.4
  4.6 0.8 %copy-done.4 = bf16[1,1,64,512]{3,2,1,0:T(8,128)(2,1)S(1)} copy-done((bf16[1,1,64,512]{3,2,1,0:T(8,128)(2,1)S(1)}, bf16[1,1,64,512]{3,2,1,0:T(8,128)(2,1)}, u32[]{:S(2)}) %copy-start.4) | copy-done | bytes 65560
  5.4 0.0 copy-start.5
  5.4 0.8 %copy-done.5 = bf16[1,1,64,512]{3,2,1,0:T(8,128)(2,1)S(1)} copy-done((bf16[1,1,64,512]{3,2,1,0:T(8,128)(2,1)S(1)}, bf16[1,1,64,512]{3,2,1,0:T(8,128)(2,1)}, u32[]{:S(2)}) %copy-start.5) | copy-done | bytes 65560
  6.3 0.0 copy-start.6
  6.3 0.8 %copy-done.6 = bf16[1,1,64,512]{3,2,1,0:T(8,128)(2,1)S(1)} copy-done((bf16[1,1,64,512]{3,2,1,0:T(8,128)(2,1)S(1)}, bf16[1,1,64,512]{3,2,1,0:T(8,128)(2,1)}, u32[]{:S(2)}) %copy-start.6) | copy-done | bytes 65560
  7.1 0.0 copy-start.7
  7.1 0.7 %copy-done.7 = bf16[1,4096]{1,0:T(2,128)(2,1)S(1)} copy-done((bf16[1,4096]{1,0:T(2,128)(2,1)S(1)}, bf16[1,4096]{1,0:T(2,128)(2,1)}, u32[]{:S(2)}) %copy-start.7) | copy-done | bytes 8216
  7.8 35.5 %shard_map.119 = (bf16[64,4096]{1,0:T(8,128)(2,1)S(1)}, bf16[64,4096]{1,0:T(8,128)(2,1)S(1)}, bf16[64,512]{1,0:T(8,128)(2,1)S(1)}, bf16[64,512]{1,0:T(8,128)(2,1)S(1)}, f32[1,1024]{1,0:T(1,128)S(1)}) custom-call(bf16[64,4096]{1,0:T(8,128)(2,1)S(1)} %bitcast.15, bf16[64,512]{1,0:T(8,128)(2,1)S(1)} %bitcast.18, bf16[64,512]{1,0:T(8,128)(2,1)S(1)} %bitcast.19, ...), custom_call_target="tpu_custom_call" | custom-call | flops 939524096 | bytes 2097152 | tf_op jit(solution)/shard_map/pallas_call | solution.py:305
  43.4 0.8 %copy.18 = bf16[1,1,64,4096]{3,2,1,0:T(8,128)(2,1)} copy(bf16[1,1,64,4096]{3,2,1,0:T(8,128)(2,1)S(1)} %bitcast.12) | data formatting | bytes 1048576
  44.2 0.8 %copy.19 = bf16[1,1,64,4096]{3,2,1,0:T(8,128)(2,1)} copy(bf16[1,1,64,4096]{3,2,1,0:T(8,128)(2,1)S(1)} %bitcast.11) | data formatting | bytes 1048576
  44.9 0.6 %copy.20 = bf16[1,1,64,512]{3,2,1,0:T(8,128)(2,1)} copy(bf16[1,1,64,512]{3,2,1,0:T(8,128)(2,1)S(1)} %bitcast.14) | data formatting | bytes 131072
  45.6 0.6 %copy.21 = bf16[1,1,64,512]{3,2,1,0:T(8,128)(2,1)} copy(bf16[1,1,64,512]{3,2,1,0:T(8,128)(2,1)S(1)} %bitcast.13) | data formatting | bytes 131072
  46.2 0.6 %copy.22 = f32[1,1024]{1,0:T(1,128)} copy(f32[1,1024]{1,0:T(1,128)S(1)} %get-tuple-element.24) | data formatting | bytes 8192
Async XLA Ops:
  0.6 1.0 %copy-start = (bf16[1,1,64,4096]{3,2,1,0:T(8,128)(2,1)S(1)}, bf16[1,1,64,4096]{3,2,1,0:T(8,128)(2,1)}, u32[]{:S(2)}) copy-start(bf16[1,1,64,4096]{3,2,1,0:T(8,128)(2,1)} %param.8) | copy-start | bytes 1572868
  1.7 1.0 %copy-start.1 = (bf16[1,1,64,4096]{3,2,1,0:T(8,128)(2,1)S(1)}, bf16[1,1,64,4096]{3,2,1,0:T(8,128)(2,1)}, u32[]{:S(2)}) copy-start(bf16[1,1,64,4096]{3,2,1,0:T(8,128)(2,1)} %param.11) | copy-start | bytes 1572868
  2.7 1.0 %copy-start.2 = (bf16[1,1,64,4096]{3,2,1,0:T(8,128)(2,1)S(1)}, bf16[1,1,64,4096]{3,2,1,0:T(8,128)(2,1)}, u32[]{:S(2)}) copy-start(bf16[1,1,64,4096]{3,2,1,0:T(8,128)(2,1)} %param.14) | copy-start | bytes 1572868
  3.8 0.8 %copy-start.3 = (bf16[1,1,64,512]{3,2,1,0:T(8,128)(2,1)S(1)}, bf16[1,1,64,512]{3,2,1,0:T(8,128)(2,1)}, u32[]{:S(2)}) copy-start(bf16[1,1,64,512]{3,2,1,0:T(8,128)(2,1)} %param.9) | copy-start | bytes 196612
  4.6 0.8 %copy-start.4 = (bf16[1,1,64,512]{3,2,1,0:T(8,128)(2,1)S(1)}, bf16[1,1,64,512]{3,2,1,0:T(8,128)(2,1)}, u32[]{:S(2)}) copy-start(bf16[1,1,64,512]{3,2,1,0:T(8,128)(2,1)} %param.10) | copy-start | bytes 196612
  5.4 0.8 %copy-start.5 = (bf16[1,1,64,512]{3,2,1,0:T(8,128)(2,1)S(1)}, bf16[1,1,64,512]{3,2,1,0:T(8,128)(2,1)}, u32[]{:S(2)}) copy-start(bf16[1,1,64,512]{3,2,1,0:T(8,128)(2,1)} %param.12) | copy-start | bytes 196612
  6.3 0.8 %copy-start.6 = (bf16[1,1,64,512]{3,2,1,0:T(8,128)(2,1)S(1)}, bf16[1,1,64,512]{3,2,1,0:T(8,128)(2,1)}, u32[]{:S(2)}) copy-start(bf16[1,1,64,512]{3,2,1,0:T(8,128)(2,1)} %param.13) | copy-start | bytes 196612
  7.1 0.7 %copy-start.7 = (bf16[1,4096]{1,0:T(2,128)(2,1)S(1)}, bf16[1,4096]{1,0:T(2,128)(2,1)}, u32[]{:S(2)}) copy-start(bf16[1,4096]{1,0:T(2,128)(2,1)} %gain_ref.1) | copy-start | bytes 24580

commit v2 on v1

--- a/solution.py
+++ b/solution.py
@@ -16,6 +16,7 @@
 EPS = 1e-05
 SCALE = 1.0 / math.sqrt(HD)
 SCALE_LOG2 = SCALE * math.log2(math.e)
+VMEM_LIMIT = 60 * 1024 * 1024
 MESH = pl.DeviceIdType.MESH
 F32 = jnp.float32
 BF16 = jnp.bfloat16
@@ -31,9 +32,9 @@
 
 def kernel(
     n, pipes, replicas, rows,
-    q1_in, k1_in, v1_in, q2_in, k2_in, v2_in, go_in, gain_ref,
+    q1_in, k1_in, v1_in, q2_in, k2_in, v2_in, go_in, gain_in,
     next_out, gq_out, gk_out, gv_out, gain_out,
-    q1, q2, up, k1, v1, k2, v2, probs, o1, o2, grad, gq, part, own, land,
+    gain_ref, q1, q2, up, k1, v1, k2, v2, probs, o1, o2, grad, gq, part, own, land,
     gpart, gland, gshare,
     local_sem, kv_send, kv_recv, part_send, part_recv, out_sem,
     pipe_send, pipe_recv, gain_send, gain_recv, rep_send, rep_recv,
@@ -55,6 +56,7 @@
                 (q2_in, q2),
                 (k2_in, k2.at[block(me)]),
                 (v2_in, v2.at[block(me)]),
+                (gain_in, gain_ref),
                 (q1_in, q1),
                 (k1_in, k1.at[block(me)]),
                 (v1_in, v1.at[block(me)]),
@@ -145,7 +147,7 @@
     def inverse_of(squares):
         return lax.rsqrt(jnp.sum(squares, axis=-1, keepdims=True) * (1.0 / WIDTH) + EPS)
 
-    for copy in locals_[:3]:
+    for copy in locals_[:4]:
         copy.wait()
     squares = jnp.zeros((rows, HD), F32)
     for g in range(KVH):
@@ -232,7 +234,7 @@
     for d in range(1, replicas):
         replica_copy(d, replica).start()
 
-    for copy in locals_[3:]:
+    for copy in locals_[4:]:
         copy.wait()
     squares = jnp.zeros((rows, HD), F32)
     for g in range(KVH):
@@ -291,12 +293,27 @@
     normed.wait()
 
 
+def write_out(nxt, gq, own, land, gshare, nxt_out, gq_out, gk_out, gv_out, gain_out, sems):
+    copies = [
+        pltpu.make_async_copy(nxt, nxt_out, sems.at[0]),
+        pltpu.make_async_copy(gq, gq_out, sems.at[1]),
+        pltpu.make_async_copy(own, gk_out, sems.at[2]),
+        pltpu.make_async_copy(land, gv_out, sems.at[3]),
+        pltpu.make_async_copy(gshare, gain_out, sems.at[4]),
+    ]
+    for copy in copies:
+        copy.start()
+    for copy in copies:
+        copy.wait()
+
+
 def local(n, pipes, replicas, q1, k1, v1, q2, k2, v2, go, gain):
     rows = q1.shape[2]
     length = n * rows
     share = QH // n
     args = [x[0, 0] for x in (q1, k1, v1, q2, k2, v2, go)] + [gain]
     anywhere = pl.BlockSpec(memory_space=pl.ANY)
+    hbm = pl.BlockSpec(memory_space=pltpu.HBM)
     vmem = pl.BlockSpec(memory_space=pltpu.VMEM)
     wide = pltpu.VMEM((rows, WIDTH), BF16)
     keys = pltpu.VMEM((length, KVH * HD), BF16)
@@ -311,9 +328,10 @@
             jax.ShapeDtypeStruct((rows, KVH * HD), BF16),
             jax.ShapeDtypeStruct((1, WIDTH // n), F32),
         ),
-        in_specs=[anywhere] * 7 + [vmem],
+        in_specs=[hbm] * 8,
         out_specs=(anywhere, anywhere, vmem, vmem, vmem),
         scratch_shapes=[
+            pltpu.VMEM((1, WIDTH), BF16),
             wide, wide, wide, keys, keys, keys, keys,
             pltpu.VMEM((KVH, HPG * rows, length), F32),
             wide, wide, wide, wide,
@@ -323,7 +341,7 @@
             pltpu.VMEM((n, share, HD), F32),
             pltpu.VMEM((n - 1, share, HD), F32),
             pltpu.VMEM((replicas, share, HD), F32),
-            dma((6,)),
+            dma((7,)),
             dma((4, KVH, n - 1)), dma((4, KVH, n - 1)),
             dma((KVH, n - 1)), dma((KVH, n - 1)),
             dma((KVH,)),
@@ -332,11 +350,18 @@
             dma((replicas - 1,)), dma((replicas - 1,)),
         ],
         compiler_params=pltpu.CompilerParams(
-            collective_id=0, has_side_effects=True, vmem_limit_bytes=48 * 1024 * 1024
+            collective_id=0, has_side_effects=True, vmem_limit_bytes=VMEM_LIMIT
         ),
         cost_estimate=pl.CostEstimate(flops=flops, bytes_accessed=8 * rows * WIDTH, transcendentals=0),
     )(*args)
-    nxt, gq, gk, gv, gg = outs
+    nxt, gq, gk, gv, gg = pl.pallas_call(
+        write_out,
+        out_shape=tuple(jax.ShapeDtypeStruct(x.shape, x.dtype) for x in outs),
+        in_specs=[anywhere] * 5,
+        out_specs=(hbm,) * 5,
+        scratch_shapes=[dma((5,))],
+        compiler_params=pltpu.CompilerParams(vmem_limit_bytes=VMEM_LIMIT),
+    )(*outs)
     return nxt[None, None], gq[None, None], gk[None, None], gv[None, None], gg
 
 

time: 47.3 us -> 73.8 us (1.56)
  Pallas kernels: 35.5 us -> 73 us
  local copies, waits for them, and re-layouts: 10.6 us -> 0 us
    pallas_call x0 -> x1, Pallas kernels: none -> 37 us  [local(): pl.pallas_call(write_out, out_shape=tuple((jax.ShapeDtypeStruct(x.shape,...]
    unnamed x21 -> x0, local copies, waits for them, and re-layouts: 10.6 us -> none
where the time goes in v2:
time: 73.8 us; the launch traced here: 73.7 us
  Pallas kernels  73 us (99%)
    pallas_call x1, Pallas kernels, local(): pl.pallas_call(write_out, out_shape=tuple((jax.ShapeDtypeStruct(x.shape,...  37 us
    pallas_call x1, Pallas kernels, local(): pl.pallas_call(functools.partial(kernel, n, pipes, replicas, rows), out_s...  36 us

profile of v2, /device:TPU:0, one launch (start us, length us, event | category | flops | bytes accessed | tf_op | source)
XLA Modules:
  0.0 73.7 jit_solution(17757783572130253722)
XLA Ops:
  0.6 36.0 %shard_map.119 = (bf16[64,4096]{1,0:T(8,128)(2,1)}, bf16[64,4096]{1,0:T(8,128)(2,1)}, bf16[64,512]{1,0:T(8,128)(2,1)}, bf16[64,512]{1,0:T(8,128)(2,1)}, f32[1,1024]{1,0:T(1,128)}) custom-call(bf16[64,4096]{1,0:T(8,128)(2,1)} %bitcast.11, bf16[64,512]{1,0:T(8,128)(2,1)} %bitcast.16, bf16[64,512]{1,0:T(8,128)(2,1)} %bitcast.17, bf16[64,4096]{1,0:T(8,128)(2,1)} %bitcast.12, ...), custom_call_target="tpu_custom_call" | custom-call | flops 939524096 | bytes 2097152 | tf_op jit(solution)/shard_map/pallas_call | solution.py:322
  36.7 37.0 %shard_map.120 = (bf16[64,4096]{1,0:T(8,128)(2,1)}, bf16[64,4096]{1,0:T(8,128)(2,1)}, bf16[64,512]{1,0:T(8,128)(2,1)}, bf16[64,512]{1,0:T(8,128)(2,1)}, f32[1,1024]{1,0:T(1,128)}) custom-call(bf16[64,4096]{1,0:T(8,128)(2,1)} %get-tuple-element.15.nxt, bf16[64,4096]{1,0:T(8,128)(2,1)} %get-tuple-element.16.gq, bf16[64,512]{1,0:T(8,128)(2,1)} %get-tuple-element.17.own, ...), custom_call_target="tpu_custom_call" | custom-call | tf_op jit(solution)/shard_map/pallas_call | solution.py:357

commit v3 on v2

--- a/solution.py
+++ b/solution.py
@@ -86,29 +86,41 @@
     pl.semaphore_wait(barrier, n - 1 + replicas - 1 + 2)
 
     def kv_copy(array, g, d, source):
-        src = (k2_in, v2_in, k1_in, v1_in)[array]
+        own_block = (k2_in, v2_in, k1_in, v1_in)[array]
         dst = (k2, v2, k1, v1)[array]
+        lanes = head(g) if array < 2 else slice(0, KVH * HD)
+        src = own_block.at[:, lanes] if d <= 2 else dst.at[block(source), lanes]
         return pltpu.make_async_remote_copy(
-            src_ref=src.at[:, head(g)],
-            dst_ref=dst.at[block(source), head(g)],
+            src_ref=src,
+            dst_ref=dst.at[block(source), lanes],
             send_sem=kv_send.at[array, g, d - 1],
             recv_sem=kv_recv.at[array, g, d - 1],
-            device_id={"seq": lax.rem(me + d, n)},
+            device_id={"seq": lax.rem(me + (d if d <= 2 else 1), n)},
             device_id_type=MESH,
         )
 
     def kv_start(arrays, g):
-        for d in range(n - 1, 0, -1):
+        for d in range(min(2, n - 1), 0, -1):
 
             @pl.when(me + d < n)
             def _():
                 for array in arrays:
                     kv_copy(array, g, d, me).start()
 
+    def kv_forward(arrays, g):
+        for d in range(2, n - 1):
+
+            @pl.when(jnp.logical_and(me >= d, me + 1 < n))
+            def _():
+                for array in arrays:
+                    kv_copy(array, g, d, me - d).wait_recv()
+                    kv_copy(array, g, d + 1, me - d).start()
+
     def kv_wait(arrays, g):
         for d in range(1, n):
-
-            @pl.when(me >= d)
+            waits = me >= d if d == 1 else me == n - 1
+
+            @pl.when(waits)
             def _():
                 for array in arrays:
                     kv_copy(array, g, d, me - d).wait_recv()
@@ -120,8 +132,6 @@
         device_id={"pipe": behind}, device_id_type=MESH,
     )
     upstream.start()
-    for g in range(KVH):
-        kv_start((2, 3), g)
 
     token = me * rows + lax.broadcasted_iota(jnp.int32, (rows, length), 0)
     allowed = (lax.broadcasted_iota(jnp.int32, (rows, length), 1) <= token)[None]
@@ -150,7 +160,12 @@
     for copy in locals_[:4]:
         copy.wait()
     squares = jnp.zeros((rows, HD), F32)
-    for g in range(KVH):
+    kv_forward((0, 1), 0)
+    for g in range(KVH):
+        if g + 1 < KVH:
+            kv_forward((0, 1), g + 1)
+        if g + 2 == KVH:
+            kv_start((2, 3), 0)
         kv_wait((0, 1), g)
         prob, more = forward(q2, k2, v2, o2, g)
         probs[g] = prob
@@ -186,8 +201,20 @@
         return pltpu.make_async_remote_copy(
             src_ref=part.at[target, g], dst_ref=land.at[d - 1, g],
             send_sem=part_send.at[g, d - 1], recv_sem=part_recv.at[g, d - 1],
-            device_id={"seq": target}, device_id_type=MESH,
-        )
+            device_id={"seq": lax.rem(me + n - (d if d <= 2 else 1), n)}, device_id_type=MESH,
+        )
+
+    def part_relay(g):
+        for d in range(n - 2, 1, -1):
+
+            @pl.when(jnp.logical_and(me >= d, me + 1 < n))
+            def _():
+                target = me - d
+                part_copy(g, d + 1, target).wait_recv()
+                for which in range(2):
+                    total = own[g, which, block(target), :] + land[d, g, which].astype(F32)
+                    part[target, g, which] = total.astype(BF16)
+                part_copy(g, d, target).start()
 
     def gq_copy(g):
         lanes = slice(g * HPG * HD, (g + 1) * HPG * HD)
@@ -208,7 +235,7 @@
                 part[b, g, which] = value[b * rows : (b + 1) * rows].astype(BF16)
         for d in range(n - 1, 0, -1):
 
-            @pl.when(me >= d)
+            @pl.when(me >= 1 if d == 1 else me == n - 1)
             def _():
                 part_copy(g, d, me - d).start()
 
@@ -216,6 +243,8 @@
         for h in range(HPG):
             gq[:, head(g * HPG + h)] = grad_query[h * rows : (h + 1) * rows]
         gq_copy(g).start()
+        if g == 1:
+            kv_forward((2, 3), 0)
 
     for d in range(1, n):
         gain_copy(d).wait_recv()
@@ -237,8 +266,9 @@
     for copy in locals_[4:]:
         copy.wait()
     squares = jnp.zeros((rows, HD), F32)
-    for g in range(KVH):
-        kv_wait((2, 3), g)
+    kv_wait((2, 3), 0)
+    for g in range(KVH):
+        part_relay(g)
         prob, more = forward(q1, k1, v1, o1, g)
         squares += more
     inverse = inverse_of(squares)
@@ -252,7 +282,7 @@
     normed.start()
 
     for g in range(KVH):
-        for d in range(1, n):
+        for d in range(1, min(2, n - 1) + 1):
 
             @pl.when(me + d < n)
             def _():
@@ -272,12 +302,15 @@
         gain_out[:, head(h)] = total[h : h + 1]
 
     for d in range(1, n):
-
-        @pl.when(me + d < n)
+        sent = me + d < n if d <= 2 else jnp.logical_and(me + 1 >= d, me + 1 < n)
+
+        @pl.when(sent)
         def _():
             for g in range(KVH):
-                for array in range(4):
-                    kv_copy(array, g, d, me).wait_send()
+                for array in (0, 1):
+                    kv_copy(array, g, d, me if d <= 2 else me + 1 - d).wait_send()
+            for array in (2, 3):
+                kv_copy(array, 0, d, me if d <= 2 else me + 1 - d).wait_send()
 
         @pl.when(me >= d)
         def _():
@@ -293,18 +326,19 @@
     normed.wait()
 
 
-def write_out(nxt, gq, own, land, gshare, nxt_out, gq_out, gk_out, gv_out, gain_out, sems):
-    copies = [
-        pltpu.make_async_copy(nxt, nxt_out, sems.at[0]),
-        pltpu.make_async_copy(gq, gq_out, sems.at[1]),
-        pltpu.make_async_copy(own, gk_out, sems.at[2]),
-        pltpu.make_async_copy(land, gv_out, sems.at[3]),
-        pltpu.make_async_copy(gshare, gain_out, sems.at[4]),
-    ]
-    for copy in copies:
-        copy.start()
-    for copy in copies:
-        copy.wait()
+def write_out(*refs):
+    count = len(refs) // 3
+    sources, targets, held = refs[:count], refs[count : 2 * count], refs[2 * count : 3 * count]
+    in_sem, out_sem = refs[3 * count :]
+    reads = [pltpu.make_async_copy(sources[i], held[i], in_sem.at[i]) for i in range(count)]
+    writes = [pltpu.make_async_copy(held[i], targets[i], out_sem.at[i]) for i in range(count)]
+    for read in reads:
+        read.start()
+    for read, write in zip(reads, writes):
+        read.wait()
+        write.start()
+    for write in writes:
+        write.wait()
 
 
 def local(n, pipes, replicas, q1, k1, v1, q2, k2, v2, go, gain):
@@ -359,7 +393,7 @@
         out_shape=tuple(jax.ShapeDtypeStruct(x.shape, x.dtype) for x in outs),
         in_specs=[anywhere] * 5,
         out_specs=(hbm,) * 5,
-        scratch_shapes=[dma((5,))],
+        scratch_shapes=[pltpu.VMEM(x.shape, x.dtype) for x in outs] + [dma((5,)), dma((5,))],
         compiler_params=pltpu.CompilerParams(vmem_limit_bytes=VMEM_LIMIT),
     )(*outs)
     return nxt[None, None], gq[None, None], gk[None, None], gv[None, None], gg

time: 73.8 us -> 35.4 us (0.48)
  Pallas kernels: 73 us -> 34.6 us
    pallas_call x1, Pallas kernels: 37 us -> 2.13 us  [local(): pl.pallas_call(write_out, out_shape=tuple((jax.ShapeDtypeStruct(x.shape,...]
    pallas_call x1, Pallas kernels: 36 us -> 32.5 us  [local(): pl.pallas_call(functools.partial(kernel, n, pipes, replicas, rows), out_s...]
where the time goes in v3:
time: 35.4 us; the launch traced here: 35.3 us
  Pallas kernels  34.6 us (98%)
  between operations  0.64 us (2%)
    pallas_call x1, Pallas kernels, local(): pl.pallas_call(functools.partial(kernel, n, pipes, replicas, rows), out_s...  32.5 us
    pallas_call x1, Pallas kernels, local(): pl.pallas_call(write_out, out_shape=tuple((jax.ShapeDtypeStruct(x.shape,...  2.13 us

profile of v3, /device:TPU:0, one launch (start us, length us, event | category | flops | bytes accessed | tf_op | source)
XLA Modules:
  0.0 35.3 jit_solution(1760887903527989188)
XLA Ops:
  0.6 32.5 %shard_map.119 = (bf16[64,4096]{1,0:T(8,128)(2,1)}, bf16[64,4096]{1,0:T(8,128)(2,1)}, bf16[64,512]{1,0:T(8,128)(2,1)}, bf16[64,512]{1,0:T(8,128)(2,1)}, f32[1,1024]{1,0:T(1,128)}) custom-call(bf16[64,4096]{1,0:T(8,128)(2,1)} %bitcast.11, bf16[64,512]{1,0:T(8,128)(2,1)} %bitcast.16, bf16[64,512]{1,0:T(8,128)(2,1)} %bitcast.17, bf16[64,4096]{1,0:T(8,128)(2,1)} %bitcast.12, ...), custom_call_target="tpu_custom_call" | custom-call | flops 939524096 | bytes 2097152 | tf_op jit(solution)/shard_map/pallas_call | solution.py:356
  33.2 2.1 %shard_map.120 = (bf16[64,4096]{1,0:T(8,128)(2,1)}, bf16[64,4096]{1,0:T(8,128)(2,1)}, bf16[64,512]{1,0:T(8,128)(2,1)}, bf16[64,512]{1,0:T(8,128)(2,1)}, f32[1,1024]{1,0:T(1,128)}) custom-call(bf16[64,4096]{1,0:T(8,128)(2,1)} %get-tuple-element.15.refs_0_, bf16[64,4096]{1,0:T(8,128)(2,1)} %get-tuple-element.16.refs_1_, ...), custom_call_target="tpu_custom_call" | custom-call | tf_op jit(solution)/shard_map/pallas_call | solution.py:391

commit v4 on v3

--- a/solution.py
+++ b/solution.py
@@ -17,6 +17,7 @@
 SCALE = 1.0 / math.sqrt(HD)
 SCALE_LOG2 = SCALE * math.log2(math.e)
 VMEM_LIMIT = 60 * 1024 * 1024
+HALF = KVH * HD // 2
 MESH = pl.DeviceIdType.MESH
 F32 = jnp.float32
 BF16 = jnp.bfloat16
@@ -34,7 +35,7 @@
     n, pipes, replicas, rows,
     q1_in, k1_in, v1_in, q2_in, k2_in, v2_in, go_in, gain_in,
     next_out, gq_out, gk_out, gv_out, gain_out,
-    gain_ref, q1, q2, up, k1, v1, k2, v2, probs, o1, o2, grad, gq, part, own, land,
+    gain_ref, q1, q2, up, k1, v1, k2, v2, probs, scores_grad, o1, o2, grad, gq, part, own, land,
     gpart, gland, gshare,
     local_sem, kv_send, kv_recv, part_send, part_recv, out_sem,
     pipe_send, pipe_recv, gain_send, gain_recv, rep_send, rep_recv,
@@ -88,7 +89,7 @@
     def kv_copy(array, g, d, source):
         own_block = (k2_in, v2_in, k1_in, v1_in)[array]
         dst = (k2, v2, k1, v1)[array]
-        lanes = head(g) if array < 2 else slice(0, KVH * HD)
+        lanes = head(g) if array < 2 else slice(g * HALF, (g + 1) * HALF)
         src = own_block.at[:, lanes] if d <= 2 else dst.at[block(source), lanes]
         return pltpu.make_async_remote_copy(
             src_ref=src,
@@ -99,10 +100,10 @@
             device_id_type=MESH,
         )
 
-    def kv_start(arrays, g):
+    def kv_start(arrays, g, low, high):
         for d in range(min(2, n - 1), 0, -1):
 
-            @pl.when(me + d < n)
+            @pl.when(jnp.logical_and(me >= low, me < jnp.minimum(high, n - d)))
             def _():
                 for array in arrays:
                     kv_copy(array, g, d, me).start()
@@ -126,7 +127,7 @@
                     kv_copy(array, g, d, me - d).wait_recv()
 
     for g in range(KVH):
-        kv_start((0, 1), g)
+        kv_start((0, 1), g, 0, n)
     upstream = pltpu.make_async_remote_copy(
         src_ref=go_in, dst_ref=up, send_sem=pipe_send.at[0], recv_sem=pipe_recv.at[0],
         device_id={"pipe": behind}, device_id_type=MESH,
@@ -164,8 +165,6 @@
     for g in range(KVH):
         if g + 1 < KVH:
             kv_forward((0, 1), g + 1)
-        if g + 2 == KVH:
-            kv_start((2, 3), 0)
         kv_wait((0, 1), g)
         prob, more = forward(q2, k2, v2, o2, g)
         probs[g] = prob
@@ -194,6 +193,8 @@
             device_id={"seq": owner}, device_id_type=MESH,
         )
 
+    for half in range(2):
+        kv_start((2, 3), half, 1, n)
     for d in range(1, n):
         gain_copy(d).start()
 
@@ -227,6 +228,7 @@
         dots = jnp.sum(grads.astype(F32) * outs.astype(F32), axis=-1, keepdims=True)
         grad_weights = dot(grads, v2[:, head(g)], (1, 1))
         grad_scores = (prob * (grad_weights - dots) * SCALE).astype(BF16)
+        scores_grad[g] = grad_scores
         for which, value in enumerate(
             (dot(grad_scores, stack(q2, g), (0, 0)), dot(prob.astype(BF16), grads, (0, 0)))
         ):
@@ -239,12 +241,17 @@
             def _():
                 part_copy(g, d, me - d).start()
 
-        grad_query = dot(grad_scores, k2[:, head(g)], (1, 0)).astype(BF16)
+        if g == 1:
+            for half in range(2):
+                kv_start((2, 3), half, 0, 1)
+        if g >= 2:
+            kv_forward((2, 3), g - 2)
+
+    for g in range(KVH):
+        grad_query = dot(scores_grad[g], k2[:, head(g)], (1, 0)).astype(BF16)
         for h in range(HPG):
             gq[:, head(g * HPG + h)] = grad_query[h * rows : (h + 1) * rows]
         gq_copy(g).start()
-        if g == 1:
-            kv_forward((2, 3), 0)
 
     for d in range(1, n):
         gain_copy(d).wait_recv()
@@ -266,20 +273,27 @@
     for copy in locals_[4:]:
         copy.wait()
     squares = jnp.zeros((rows, HD), F32)
-    kv_wait((2, 3), 0)
     for g in range(KVH):
         part_relay(g)
+    for g in range(KVH):
+        if g % 2 == 0:
+            kv_wait((2, 3), g // 2)
         prob, more = forward(q1, k1, v1, o1, g)
         squares += more
     inverse = inverse_of(squares)
-    for h in range(QH):
-        gain = gain_ref[:, head(h)].astype(F32)
-        o1[:, head(h)] = (gain * o1[:, head(h)].astype(F32) * inverse).astype(BF16)
-    normed = pltpu.make_async_remote_copy(
-        src_ref=o1, dst_ref=next_out, send_sem=pipe_send.at[1], recv_sem=pipe_recv.at[1],
-        device_id={"pipe": ahead}, device_id_type=MESH,
-    )
-    normed.start()
+    def normed_copy(g):
+        lanes = slice(g * HPG * HD, (g + 1) * HPG * HD)
+        return pltpu.make_async_remote_copy(
+            src_ref=o1.at[:, lanes], dst_ref=next_out.at[:, lanes],
+            send_sem=pipe_send.at[1 + g], recv_sem=pipe_recv.at[1 + g],
+            device_id={"pipe": ahead}, device_id_type=MESH,
+        )
+
+    for g in range(KVH):
+        for h in range(g * HPG, (g + 1) * HPG):
+            gain = gain_ref[:, head(h)].astype(F32)
+            o1[:, head(h)] = (gain * o1[:, head(h)].astype(F32) * inverse).astype(BF16)
+        normed_copy(g).start()
 
     for g in range(KVH):
         for d in range(1, min(2, n - 1) + 1):
@@ -309,8 +323,9 @@
             for g in range(KVH):
                 for array in (0, 1):
                     kv_copy(array, g, d, me if d <= 2 else me + 1 - d).wait_send()
-            for array in (2, 3):
-                kv_copy(array, 0, d, me if d <= 2 else me + 1 - d).wait_send()
+            for half in range(2):
+                for array in (2, 3):
+                    kv_copy(array, half, d, me if d <= 2 else me + 1 - d).wait_send()
 
         @pl.when(me >= d)
         def _():
@@ -323,7 +338,7 @@
     upstream.wait_send()
     for g in range(KVH):
         gq_copy(g).wait()
-    normed.wait()
+        normed_copy(g).wait()
 
 
 def write_out(*refs):
@@ -368,6 +383,7 @@
             pltpu.VMEM((1, WIDTH), BF16),
             wide, wide, wide, keys, keys, keys, keys,
             pltpu.VMEM((KVH, HPG * rows, length), F32),
+            pltpu.VMEM((KVH, HPG * rows, length), BF16),
             wide, wide, wide, wide,
             pltpu.VMEM((n, KVH, 2, rows, HD), BF16),
             pltpu.VMEM((KVH, 2, length, HD), F32),
@@ -379,7 +395,7 @@
             dma((4, KVH, n - 1)), dma((4, KVH, n - 1)),
             dma((KVH, n - 1)), dma((KVH, n - 1)),
             dma((KVH,)),
-            dma((2,)), dma((2,)),
+            dma((1 + KVH,)), dma((1 + KVH,)),
             dma((n - 1,)), dma((n - 1,)),
             dma((replicas - 1,)), dma((replicas - 1,)),
         ],

time: 35.4 us -> 34.5 us (0.975)
  Pallas kernels: 34.6 us -> 33.7 us
    pallas_call x1, Pallas kernels: 32.5 us -> 31.5 us  [local(): pl.pallas_call(functools.partial(kernel, n, pipes, replicas, rows), out_s...]
where the time goes in v4:
time: 34.5 us; the launch traced here: 34.3 us
  Pallas kernels  33.7 us (98%)
  between operations  0.64 us (2%)
    pallas_call x1, Pallas kernels, local(): pl.pallas_call(functools.partial(kernel, n, pipes, replicas, rows), out_s...  31.5 us
    pallas_call x1, Pallas kernels, local(): pl.pallas_call(write_out, out_shape=tuple((jax.ShapeDtypeStruct(x.shape,...  2.13 us

profile of v4, /device:TPU:0, one launch (start us, length us, event | category | flops | bytes accessed | tf_op | source)
XLA Modules:
  0.0 34.3 jit_solution(7936975409375668504)
XLA Ops:
  0.6 31.5 %shard_map.119 = (bf16[64,4096]{1,0:T(8,128)(2,1)}, bf16[64,4096]{1,0:T(8,128)(2,1)}, bf16[64,512]{1,0:T(8,128)(2,1)}, bf16[64,512]{1,0:T(8,128)(2,1)}, f32[1,1024]{1,0:T(1,128)}) custom-call(bf16[64,4096]{1,0:T(8,128)(2,1)} %bitcast.11, bf16[64,512]{1,0:T(8,128)(2,1)} %bitcast.16, bf16[64,512]{1,0:T(8,128)(2,1)} %bitcast.17, bf16[64,4096]{1,0:T(8,128)(2,1)} %bitcast.12, ...), custom_call_target="tpu_custom_call" | custom-call | flops 939524096 | bytes 2097152 | tf_op jit(solution)/shard_map/pallas_call | solution.py:371
  32.2 2.1 %shard_map.120 = (bf16[64,4096]{1,0:T(8,128)(2,1)}, bf16[64,4096]{1,0:T(8,128)(2,1)}, bf16[64,512]{1,0:T(8,128)(2,1)}, bf16[64,512]{1,0:T(8,128)(2,1)}, f32[1,1024]{1,0:T(1,128)}) custom-call(bf16[64,4096]{1,0:T(8,128)(2,1)} %get-tuple-element.15.refs_0_, bf16[64,4096]{1,0:T(8,128)(2,1)} %get-tuple-element.16.refs_1_, ...), custom_call_target="tpu_custom_call" | custom-call | tf_op jit(solution)/shard_map/pallas_call | solution.py:407

commit v5 on v4

--- a/solution.py
+++ b/solution.py
@@ -35,7 +35,7 @@
     n, pipes, replicas, rows,
     q1_in, k1_in, v1_in, q2_in, k2_in, v2_in, go_in, gain_in,
     next_out, gq_out, gk_out, gv_out, gain_out,
-    gain_ref, q1, q2, up, k1, v1, k2, v2, probs, scores_grad, o1, o2, grad, gq, part, own, land,
+    gain_ref, q1, q2, up, k1, v1, k2, v2, bias, probs, scores_grad, o1, o2, grad, gq, part, own, land,
     gpart, gland, gshare,
     local_sem, kv_send, kv_recv, part_send, part_recv, out_sem,
     pipe_send, pipe_recv, gain_send, gain_recv, rep_send, rep_recv,
@@ -135,25 +135,30 @@
     upstream.start()
 
     token = me * rows + lax.broadcasted_iota(jnp.int32, (rows, length), 0)
-    allowed = (lax.broadcasted_iota(jnp.int32, (rows, length), 1) <= token)[None]
+    bias[...] = jnp.where(lax.broadcasted_iota(jnp.int32, (rows, length), 1) <= token, 0.0, -jnp.inf)
 
     def stack(ref, g):
         return jnp.concatenate([ref[:, head(g * HPG + h)] for h in range(HPG)], axis=0)
 
-    def forward(q, k, v, o, g):
-        scores = dot(stack(q, g), k[:, head(g)], (1, 1)).reshape(HPG, rows, length)
-        scores = jnp.where(allowed, scores, -jnp.inf)
-        highest = jnp.max(scores, axis=-1, keepdims=True)
-        exponent = jnp.exp2((scores - highest) * SCALE_LOG2)
-        prob = exponent * (1.0 / jnp.sum(exponent, axis=-1, keepdims=True))
-        prob = prob.reshape(HPG * rows, length)
-        out = dot(prob.astype(BF16), v[:, head(g)], (1, 0)).astype(BF16)
+    def forward(q, k, v, o, g, keep):
+        scores = dot(stack(q, g), k[:, head(g)], (1, 1))
+        weights = []
+        for h in range(HPG):
+            part_rows = slice(h * rows, (h + 1) * rows)
+            score = scores[part_rows] + bias[...]
+            highest = jnp.max(score, axis=-1, keepdims=True)
+            exponent = jnp.exp2((score - highest) * SCALE_LOG2)
+            prob = exponent * (1.0 / jnp.sum(exponent, axis=-1, keepdims=True))
+            if keep:
+                probs[g, part_rows, :] = prob
+            weights.append(prob.astype(BF16))
+        out = dot(jnp.concatenate(weights, axis=0), v[:, head(g)], (1, 0)).astype(BF16)
         squares = jnp.zeros((rows, HD), F32)
         for h in range(HPG):
             piece = out[h * rows : (h + 1) * rows]
             o[:, head(g * HPG + h)] = piece
             squares += piece.astype(F32) * piece.astype(F32)
-        return prob, squares
+        return squares
 
     def inverse_of(squares):
         return lax.rsqrt(jnp.sum(squares, axis=-1, keepdims=True) * (1.0 / WIDTH) + EPS)
@@ -166,9 +171,7 @@
         if g + 1 < KVH:
             kv_forward((0, 1), g + 1)
         kv_wait((0, 1), g)
-        prob, more = forward(q2, k2, v2, o2, g)
-        probs[g] = prob
-        squares += more
+        squares += forward(q2, k2, v2, o2, g, True)
     inverse = inverse_of(squares)
 
     upstream.wait_recv()
@@ -223,14 +226,21 @@
 
     for g in range(KVH):
         grads = stack(grad, g)
-        outs = stack(o2, g)
-        prob = probs[g]
-        dots = jnp.sum(grads.astype(F32) * outs.astype(F32), axis=-1, keepdims=True)
         grad_weights = dot(grads, v2[:, head(g)], (1, 1))
-        grad_scores = (prob * (grad_weights - dots) * SCALE).astype(BF16)
-        scores_grad[g] = grad_scores
+        weights, grad_scores = [], []
+        for h in range(HPG):
+            part_rows = slice(h * rows, (h + 1) * rows)
+            product = grad[:, head(g * HPG + h)].astype(F32) * o2[:, head(g * HPG + h)].astype(F32)
+            dots = jnp.sum(product, axis=-1, keepdims=True)
+            prob = probs[g, part_rows, :]
+            score = (prob * (grad_weights[part_rows] - dots) * SCALE).astype(BF16)
+            scores_grad[g, part_rows, :] = score
+            grad_scores.append(score)
+            weights.append(prob.astype(BF16))
+        grad_scores = jnp.concatenate(grad_scores, axis=0)
+        weights = jnp.concatenate(weights, axis=0)
         for which, value in enumerate(
-            (dot(grad_scores, stack(q2, g), (0, 0)), dot(prob.astype(BF16), grads, (0, 0)))
+            (dot(grad_scores, stack(q2, g), (0, 0)), dot(weights, grads, (0, 0)))
         ):
             own[g, which] = value
             for b in range(n - 1):
@@ -278,8 +288,7 @@
     for g in range(KVH):
         if g % 2 == 0:
             kv_wait((2, 3), g // 2)
-        prob, more = forward(q1, k1, v1, o1, g)
-        squares += more
+        squares += forward(q1, k1, v1, o1, g, False)
     inverse = inverse_of(squares)
     def normed_copy(g):
         lanes = slice(g * HPG * HD, (g + 1) * HPG * HD)
@@ -382,6 +391,7 @@
         scratch_shapes=[
             pltpu.VMEM((1, WIDTH), BF16),
             wide, wide, wide, keys, keys, keys, keys,
+            pltpu.VMEM((rows, length), F32),
             pltpu.VMEM((KVH, HPG * rows, length), F32),
             pltpu.VMEM((KVH, HPG * rows, length), BF16),
             wide, wide, wide, wide,

time: 34.5 us -> 34.5 us (level)
  no operation moved by 1% of the time
where the time goes in v5:
time: 34.5 us; the launch traced here: 34.3 us
  Pallas kernels  33.7 us (98%)
  between operations  0.64 us (2%)
    pallas_call x1, Pallas kernels, local(): pl.pallas_call(functools.partial(kernel, n, pipes, replicas, rows), out_s...  31.5 us
    pallas_call x1, Pallas kernels, local(): pl.pallas_call(write_out, out_shape=tuple((jax.ShapeDtypeStruct(x.shape,...  2.13 us

profile of v5, /device:TPU:0, one launch (start us, length us, event | category | flops | bytes accessed | tf_op | source)
XLA Modules:
  0.0 34.3 jit_solution(15720978710897033363)
XLA Ops:
  0.6 31.5 %shard_map.119 = (bf16[64,4096]{1,0:T(8,128)(2,1)}, bf16[64,4096]{1,0:T(8,128)(2,1)}, bf16[64,512]{1,0:T(8,128)(2,1)}, bf16[64,512]{1,0:T(8,128)(2,1)}, f32[1,1024]{1,0:T(1,128)}) custom-call(bf16[64,4096]{1,0:T(8,128)(2,1)} %bitcast.11, bf16[64,512]{1,0:T(8,128)(2,1)} %bitcast.16, bf16[64,512]{1,0:T(8,128)(2,1)} %bitcast.17, bf16[64,4096]{1,0:T(8,128)(2,1)} %bitcast.12, ...), custom_call_target="tpu_custom_call" | custom-call | flops 939524096 | bytes 2097152 | tf_op jit(solution)/shard_map/pallas_call | solution.py:380
  32.2 2.1 %shard_map.120 = (bf16[64,4096]{1,0:T(8,128)(2,1)}, bf16[64,4096]{1,0:T(8,128)(2,1)}, bf16[64,512]{1,0:T(8,128)(2,1)}, bf16[64,512]{1,0:T(8,128)(2,1)}, f32[1,1024]{1,0:T(1,128)}) custom-call(bf16[64,4096]{1,0:T(8,128)(2,1)} %get-tuple-element.15.refs_0_, bf16[64,4096]{1,0:T(8,128)(2,1)} %get-tuple-element.16.refs_1_, ...), custom_call_target="tpu_custom_call" | custom-call | tf_op jit(solution)/shard_map/pallas_call | solution.py:417

commit v6 on v5

--- a/solution.py
+++ b/solution.py
@@ -84,15 +84,15 @@
             for ref in (k1, v1, k2, v2):
                 ref[b * rows : (b + 1) * rows, :] = jnp.zeros((rows, KVH * HD), BF16)
 
+    for copy in locals_[:4]:
+        copy.wait()
     pl.semaphore_wait(barrier, n - 1 + replicas - 1 + 2)
 
     def kv_copy(array, g, d, source):
-        own_block = (k2_in, v2_in, k1_in, v1_in)[array]
         dst = (k2, v2, k1, v1)[array]
         lanes = head(g) if array < 2 else slice(g * HALF, (g + 1) * HALF)
-        src = own_block.at[:, lanes] if d <= 2 else dst.at[block(source), lanes]
         return pltpu.make_async_remote_copy(
-            src_ref=src,
+            src_ref=dst.at[block(source), lanes],
             dst_ref=dst.at[block(source), lanes],
             send_sem=kv_send.at[array, g, d - 1],
             recv_sem=kv_recv.at[array, g, d - 1],
@@ -163,8 +163,6 @@
     def inverse_of(squares):
         return lax.rsqrt(jnp.sum(squares, axis=-1, keepdims=True) * (1.0 / WIDTH) + EPS)
 
-    for copy in locals_[:4]:
-        copy.wait()
     squares = jnp.zeros((rows, HD), F32)
     kv_forward((0, 1), 0)
     for g in range(KVH):
@@ -196,6 +194,8 @@
             device_id={"seq": owner}, device_id_type=MESH,
         )
 
+    for copy in locals_[4:]:
+        copy.wait()
     for half in range(2):
         kv_start((2, 3), half, 1, n)
     for d in range(1, n):
@@ -262,6 +262,7 @@
         for h in range(HPG):
             gq[:, head(g * HPG + h)] = grad_query[h * rows : (h + 1) * rows]
         gq_copy(g).start()
+        part_relay(g)
 
     for d in range(1, n):
         gain_copy(d).wait_recv()
@@ -280,11 +281,7 @@
     for d in range(1, replicas):
         replica_copy(d, replica).start()
 
-    for copy in locals_[4:]:
-        copy.wait()
     squares = jnp.zeros((rows, HD), F32)
-    for g in range(KVH):
-        part_relay(g)
     for g in range(KVH):
         if g % 2 == 0:
             kv_wait((2, 3), g // 2)

time: 34.5 us -> 34.3 us (level)
  no operation moved by 1% of the time
where the time goes in v6:
time: 34.3 us; the launch traced here: 34.1 us
  Pallas kernels  33.5 us (98%)
  between operations  0.64 us (2%)
    pallas_call x1, Pallas kernels, local(): pl.pallas_call(functools.partial(kernel, n, pipes, replicas, rows), out_s...  31.3 us
    pallas_call x1, Pallas kernels, local(): pl.pallas_call(write_out, out_shape=tuple((jax.ShapeDtypeStruct(x.shape,...  2.13 us

profile of v6, /device:TPU:0, one launch (start us, length us, event | category | flops | bytes accessed | tf_op | source)
XLA Modules:
  0.0 34.1 jit_solution(5154013203884430999)
XLA Ops:
  0.6 31.3 %shard_map.119 = (bf16[64,4096]{1,0:T(8,128)(2,1)}, bf16[64,4096]{1,0:T(8,128)(2,1)}, bf16[64,512]{1,0:T(8,128)(2,1)}, bf16[64,512]{1,0:T(8,128)(2,1)}, f32[1,1024]{1,0:T(1,128)}) custom-call(bf16[64,4096]{1,0:T(8,128)(2,1)} %bitcast.11, bf16[64,512]{1,0:T(8,128)(2,1)} %bitcast.16, bf16[64,512]{1,0:T(8,128)(2,1)} %bitcast.17, bf16[64,4096]{1,0:T(8,128)(2,1)} %bitcast.12, ...), custom_call_target="tpu_custom_call" | custom-call | flops 939524096 | bytes 2097152 | tf_op jit(solution)/shard_map/pallas_call | solution.py:377
  32.0 2.1 %shard_map.120 = (bf16[64,4096]{1,0:T(8,128)(2,1)}, bf16[64,4096]{1,0:T(8,128)(2,1)}, bf16[64,512]{1,0:T(8,128)(2,1)}, bf16[64,512]{1,0:T(8,128)(2,1)}, f32[1,1024]{1,0:T(1,128)}) custom-call(bf16[64,4096]{1,0:T(8,128)(2,1)} %get-tuple-element.15.refs_0_, bf16[64,4096]{1,0:T(8,128)(2,1)} %get-tuple-element.16.refs_1_, ...), custom_call_target="tpu_custom_call" | custom-call | tf_op jit(solution)/shard_map/pallas_call | solution.py:414
